TPU v7x, 32 devices: a whole 2x2x4 slice. The times are simulated.
32 devices in a mesh: lat: 8 (over z, x), lev: 4 (over y, core).
Axes of the slice: x: 2, y: 2, z: 4, core: 2. Of those that a mesh axis runs over, the one named last changes fastest.
Arguments:
- tracer_dyn: bfloat16 [64, 72, 16, 1024], P(None, 'lev', 'lat'), may hold values from 0.19921875 to 5
- courant_lat: bfloat16 [72, 16, 1024], P('lev', 'lat'), may hold values from -0.44921875 to 0.44921875
- courant_lon: bfloat16 [72, 16, 1024], P('lev', 'lat'), may hold values from -0.44921875 to 0.44921875
- conv_matrix: bfloat16 [72, 72, 16384], P(None, None, ('lat', 'lev'))
- conv_mask: int32 [16384], P(('lat', 'lev')), may hold values from 0 to 1, as said below
- column_order: int32 [16384], P(('lat', 'lev')), may hold values from 0 to 511, as said below
- rain: bfloat16 [72, 16384], P(None, ('lat', 'lev')), may hold values from 0.019897461 to 1
- scav_rate: float32 [64], replicated, may hold values from 0.05 to 2
- pair_flag: int32 [16], replicated, may hold values from 0 to 1
Outputs:
- tracer_phys: bfloat16 [64, 72, 16384], P(None, None, ('lat', 'lev'))
Inputs may be any that keep to these rules, and one draw needn't show every extreme that they name: `conv_mask`: in each aligned block of 512 entries (one span) at most 256 are 1, and some block has exactly 256. `column_order`: each aligned block of 512 entries holds every number of 0 to 511 once.
All inputs are finite; a program needn't handle non-finite values.
Results may differ from a plain program's by a relative error of at most 0.005.
Values may be sent and summed in bfloat16 or wider, within the bound.
A program may use at most 128 MiB of HBM per device.

v0:
```python
import jax
import jax.numpy as jnp
from jax import lax
from jax.sharding import PartitionSpec as P


def padded_2(block, sides, width):
    for axis, dim in sides:
        count = lax.axis_size(axis)
        forward = [(i, i + 1) for i in range(count - 1)]
        backward = [(target, source) for source, target in forward]
        low = lax.ppermute(
            lax.slice_in_dim(block, block.shape[dim] - width, None, axis=dim), axis, forward
        )
        high = lax.ppermute(lax.slice_in_dim(block, 0, width, axis=dim), axis, backward)
        block = jnp.concatenate([low, block, high], axis=dim)
    return block


def shifted(value, axis, steps):
    count = lax.axis_size(axis)
    initial, last = (max(0, -steps), min(count, count - steps))
    return lax.ppermute(value, axis, [(source, source + steps) for source in range(initial, last)])


def swapped(shard, axis, apart):
    return lax.ppermute(shard, axis, [(i, i ^ 1 << apart) for i in range(lax.axis_size(axis))])


def advect_block(center, south_side, north_side, south_face, north_face, west_face):
    east_face = jnp.roll(west_face, -1, axis=-1)
    south_flux = south_face * jnp.where(south_face > 0, south_side, center)
    north_flux = north_face * jnp.where(north_face > 0, center, north_side)
    west_flux = west_face * jnp.where(west_face > 0, jnp.roll(center, 1, axis=-1), center)
    east_flux = east_face * jnp.where(east_face > 0, center, jnp.roll(center, -1, axis=-1))
    return center - (north_flux - south_flux) - (east_flux - west_flux)


def convect(matrix, tracers_bf):
    return jnp.einsum("kec,tec->tkc", matrix, tracers_bf, preferred_element_type=jnp.float32)


def local(
    tracer_dyn,
    courant_lat,
    courant_lon,
    conv_matrix,
    conv_mask,
    column_order,
    rain,
    scav_rate,
    pair_flag,
):
    n_lat = lax.axis_size("lat")
    n_lev = lax.axis_size("lev")
    tracers, lev_group, lat_dev, lon_all = tracer_dyn.shape
    lon_block = lon_all // n_lev
    padded = padded_2(tracer_dyn, (("lat", 2),), 1)
    center = tracer_dyn.astype(jnp.float32)
    south_side = padded[:, :, :-2].astype(jnp.float32)
    north_side = padded[:, :, 2:].astype(jnp.float32)
    south_face = courant_lat.astype(jnp.float32)
    above_face = shifted(courant_lat[:, :1], "lat", -1)
    north_face = jnp.concatenate([south_face[:, 1:], above_face.astype(jnp.float32)], axis=1)
    west_face = courant_lon.astype(jnp.float32)
    advected = advect_block(
        center, south_side, north_side, south_face, north_face, west_face
    ).astype(jnp.bfloat16)
    sectioned = advected.reshape(tracers, 1, lev_group, lat_dev, n_lev, lon_block)
    arrived = lax.all_to_all(sectioned, "lev", split_axis=4, concat_axis=1, tiled=True)
    physics = arrived.reshape(tracers, lev_group * n_lev, lat_dev * lon_block)
    levels = physics.shape[1]
    columns = physics.shape[2]
    placing = (jnp.arange(columns, dtype=jnp.int32)[:, None] == column_order[None, :]).astype(
        jnp.bfloat16
    )
    ordered = jnp.dot(
        physics.reshape(tracers * levels, columns), placing, preferred_element_type=jnp.float32
    )
    ordered = ordered.astype(jnp.bfloat16).reshape(tracers, levels, columns)
    ordered_f = ordered.astype(jnp.float32)
    moved = convect(conv_matrix, ordered)
    convected = jnp.where(conv_mask[None, None, :] > 0, moved, ordered_f)
    washed = (
        convected * jnp.exp(-scav_rate[:, None, None] * rain.astype(jnp.float32)[None])
    ).astype(jnp.bfloat16)
    top_bit = n_lat.bit_length() - 2
    partner = swapped(washed, "lat", top_bit)
    pair_index = lax.axis_index("lat") % (n_lat // 2) * n_lev + lax.axis_index("lev")
    flag_value = pair_flag[pair_index]
    return jnp.where(flag_value > 0, partner, washed)


def solution(mesh):
    placed = (
        P(None, "lev", "lat", None),
        P("lev", "lat", None),
        P("lev", "lat", None),
        P(None, None, ("lat", "lev")),
        P(("lat", "lev")),
        P(("lat", "lev")),
        P(None, ("lat", "lev")),
        P(),
        P(),
    )
    return jax.shard_map(
        local, mesh=mesh, in_specs=placed, out_specs=P(None, None, ("lat", "lev")), check_vma=False
    )
```

profile of v0, /device:TPU:0, one launch (start us, length us, event | category | flops | bytes accessed | tf_op | source)
XLA Modules:
  0.0 546.7 jit_solution(783367959418434285)
XLA Ops:
  1.3 9.9 %fusion.11 = (bf16[64,18,1,1024]{3,2,1,0:T(2,128)(2,1)S(1)}, bf16[64,18,1,1024]{3,2,1,0:T(2,128)(2,1)S(1)}) fusion(bf16[64,18,2,1024]{3,2,1,0:T(2,128)(2,1)} %param.9), kind=kLoop, calls=%fused_computation.29 | loop fusion | bytes 9437184 | tf_op jit(solution)/shard_map/slice | solution.py:15
  12.5 7.0 %collective-permute-start.2 = (bf16[64,18,1,1024]{3,0,2,1:T(8,128)(2,1)S(1)}, bf16[64,18,1,1024]{3,0,2,1:T(8,128)(2,1)}, u32[]{:S(2)}, u32[]{:S(2)}) collective-permute-start(bf16[64,18,1,1024]{3,0,2,1:T(8,128)(2,1)S(1)} %copy.50), channel_id=1, source_target_pairs={{0,4},{4,8},{8,12},{12,16},{16,20},{20,24},{24,28},{1,5},{5,9},{9,... | collective-permute-start | bytes 7077896 | tf_op jit(solution)/shard_map/ppermute | solution.py:12
  19.5 2.7 copy.49
  27.3 14.0 %fusion.12 = (f32[64,18,2,1023]{3,2,1,0:T(2,128)}, f32[64,18,2,1023]{3,2,1,0:T(2,128)}) fusion(bf16[64,18,2,1024]{3,2,1,0:T(2,128)(2,1)S(1)} %bitcast.20), kind=kLoop, calls=%fused_computation.30 | loop fusion | bytes 37711872 | tf_op jit(solution)/shard_map/jit(_roll_static)/slice | solution.py:35
  43.4 75.8 %collective-permute-done.2 = bf16[64,18,1,1024]{3,0,2,1:T(8,128)(2,1)} collective-permute-done((bf16[64,18,1,1024]{3,0,2,1:T(8,128)(2,1)S(1)}, bf16[64,18,1,1024]{3,0,2,1:T(8,128)(2,1)}, u32[]{:S(2)}, u32[]{:S(2)}) %collective-permute-start.2) | collective-permute-done | bytes 2359328 | tf_op jit(solution)/shard_map/ppermute | solution.py:12
  119.2 7.5 %copy.36 = bf16[64,18,1,1024]{3,2,1,0:T(2,128)(2,1)} copy(bf16[64,18,1,1024]{3,0,2,1:T(8,128)(2,1)} %collective-permute-done.2) | data formatting | bytes 4718592 | tf_op jit(solution)/shard_map/ppermute | solution.py:12
  126.7 7.5 %copy.34 = bf16[64,18,1,1024]{3,2,1,0:T(2,128)(2,1)} copy(bf16[64,18,1,1024]{3,0,2,1:T(8,128)(2,1)} %collective-permute-done.1) | data formatting | bytes 4718592 | tf_op jit(solution)/shard_map/ppermute | solution.py:15
  134.2 46.9 %fusion.9 = bf16[64,18,2,1024]{3,2,1,0:T(2,128)(2,1)} fusion(f32[64,18,2,1023]{3,2,1,0:T(2,128)} %get-tuple-element.10, f32[64,18,2,1]{3,2,1,0:T(2,128)} %get-tuple-element.12, pred[18,2,1024]{2,1,0:T(4,128)(4,1)} %get-tuple-element.13, f32[64,18,2,1]{3,2,1,0:T(2,128)} %get-tuple-element.11, f32[64,18,2,1023]{3,2,1,0:T(2,128)} %get-tuple-element.9, ...), kind=kLoop, calls=%fused_computation.15 | loop fusion | flops 56623104 | bytes 33767424 | tf_op jit(solution)/shard_map/convert_element_type | solution.py:68
  181.0 8.6 %reshape.21 = bf16[64,1,18,2,4,256]{5,4,3,2,0,1:T(4,128)(2,1)} reshape(bf16[64,18,2,1024]{3,2,1,0:T(2,128)(2,1)} %fusion.9) | data formatting | bytes 9437184 | tf_op jit(solution)/shard_map/reshape | solution.py:69
  189.6 8.1 %copy.38 = bf16[64,1,18,2,4,256]{5,3,2,0,1,4:T(2,128)(2,1)} copy(bf16[64,1,18,2,4,256]{5,4,3,2,0,1:T(4,128)(2,1)} %reshape.21) | data formatting | bytes 9437184 | tf_op jit(solution)/shard_map/reshape | solution.py:69
  197.7 5.2 all-to-all-start
  203.0 11.6 %copy.41 = bf16[72,72,512]{1,0,2:T(8,128)(2,1)} copy(bf16[72,72,512]{2,1,0:T(8,128)(2,1)} %param.12) | data formatting | bytes 10616832 | tf_op args[3]
  214.7 41.8 %all-to-all-done = bf16[64,1,18,2,4,256]{5,3,2,0,1,4:T(2,128)(2,1)} async-done(((bf16[64,1,18,2,4,256]{5,3,2,0,1,4:T(2,128)(2,1)}), bf16[64,1,18,2,4,256]{5,3,2,0,1,4:T(2,128)(2,1)}, u32[]{:S(2)}, u32[]{:S(2)}) %all-to-all-start) | async-done | bytes 4718624 | tf_op jit(solution)/shard_map/all_to_all | solution.py:70
  256.5 7.8 %copy.39 = bf16[64,4,1,18,2,1,256]{6,4,3,1,0,5,2:T(2,128)(2,1)} copy(bf16[64,4,1,18,2,1,256]{6,4,3,0,1,5,2:T(2,128)(2,1)} %bitcast.2) | data formatting | bytes 9437184 | tf_op jit(solution)/shard_map/all_to_all | solution.py:70
  264.3 3.1 copy.51
  267.4 4.4 convolution_convert_fusion
  271.8 11.2 %copy.40 = bf16[64,72,512]{1,0,2:T(8,128)(2,1)} copy(bf16[64,72,512]{2,1,0:T(8,128)(2,1)} %bitcast.22) | data formatting | bytes 9437184 | tf_op jit(solution)/shard_map/reshape | solution.py:80
  283.0 16.7 %fusion.1 = bf16[64,72,512]{1,0,2:T(8,128)(2,1)} fusion(bf16[64,72,512]{1,0,2:T(8,128)(2,1)} %copy.40, bf16[72,72,512]{1,0,2:T(8,128)(2,1)} %copy.41, f32[72,512]{0,1:T(8,128)S(1)} %copy.43, f32[64]{0:T(128)S(1)} %neg.4, pred[512]{0:T(512)(128)(4,1)S(1)} %broadcast_compare_fusion.4), kind=kOutput, calls=%fused_computation.2 | convolution fusion | flops 351535104 | bytes 14893824 | tf_op jit(solution)/shard_map/kec,tec->tkc/dot_general | solution.py:40
  299.7 11.4 %copy.44 = bf16[64,72,512]{2,1,0:T(8,128)(2,1)} copy(bf16[64,72,512]{1,0,2:T(8,128)(2,1)} %fusion.1) | data formatting | bytes 9437184 | tf_op jit(solution)/shard_map/convert_element_type | solution.py:86
  311.1 2.8 collective-permute-start.3
  315.2 201.7 %collective-permute-done.3 = bf16[64,72,512]{2,1,0:T(8,128)(2,1)} collective-permute-done((bf16[64,72,512]{2,1,0:T(8,128)(2,1)}, bf16[64,72,512]{2,1,0:T(8,128)(2,1)}, u32[]{:S(2)}, u32[]{:S(2)}) %collective-permute-start.3) | collective-permute-done | bytes 4718624 | tf_op jit(solution)/shard_map/ppermute | solution.py:27
  516.9 11.2 %copy.45 = bf16[64,72,512]{1,0,2:T(8,128)(2,1)} copy(bf16[64,72,512]{2,1,0:T(8,128)(2,1)} %collective-permute-done.3) | data formatting | bytes 9437184 | tf_op jit(solution)/shard_map/ppermute | solution.py:27
  528.1 7.2 %broadcast_select_fusion = bf16[64,72,512]{1,0,2:T(8,128)(2,1)} fusion(bf16[64,72,512]{1,0,2:T(8,128)(2,1)} %copy.45, bf16[64,72,512]{1,0,2:T(8,128)(2,1)} %fusion.1, pred[]{:T(512)} %bitcast), kind=kLoop, calls=%fused_computation.16 | loop fusion | flops 2359296 | bytes 14155777 | tf_op jit(solution)/shard_map/jit(_where)/select_n | solution.py:91
  535.3 11.4 %copy.46 = bf16[64,72,512]{2,1,0:T(8,128)(2,1)} copy(bf16[64,72,512]{1,0,2:T(8,128)(2,1)} %broadcast_select_fusion) | data formatting | bytes 9437184 | tf_op jit(solution)/shard_map/jit(_where)/select_n | solution.py:91
  (39 shorter events, 10.4 us)
Async XLA Ops:
  0.0 42.3 %collective-permute-start = (bf16[18,1,1024]{2,1,0:T(2,128)(2,1)}, bf16[18,1,1024]{2,1,0:T(2,128)(2,1)S(1)}, u32[]{:S(2)}, u32[]{:S(2)}) collective-permute-start(bf16[18,1,1024]{2,1,0:T(2,128)(2,1)} %bitcast.24), channel_id=1, source_target_pairs={{4,0},{8,4},{12,8},{16,12},{20,16},{24,20},{28,24},{5,1},{9,5},{13... | collective-permute-start | bytes 110600 | tf_op jit(solution)/shard_map/ppermute | solution.py:23
  11.2 12.6 %slice-start = ((s8[4718592]{0:T(1024)(128)(4,1)}), s8[4194304]{0:T(1024)(128)(4,1)S(1)}, s32[]{:S(2)}) async-start(s8[4718592]{0:T(1024)(128)(4,1)} %bitcast.19), calls=%async_computation.1 | async-start | bytes 8388608
  11.2 12.6 %slice-start.1 = ((s8[4718592]{0:T(1024)(128)(4,1)}), s8[524288]{0:T(1024)(128)(4,1)S(1)}, s32[]{:S(2)}) async-start(s8[4718592]{0:T(1024)(128)(4,1)} %bitcast.19), calls=%async_computation.2 | async-start | bytes 1048576
  11.2 15.1 %copy-start = (bf16[18,2,1024]{2,1,0:T(2,128)(2,1)S(1)}, bf16[18,2,1024]{2,1,0:T(2,128)(2,1)}, u32[]{:S(2)}) copy-start(bf16[18,2,1024]{2,1,0:T(2,128)(2,1)} %param.11) | copy-start | bytes 221188
  12.5 106.7 %collective-permute-start.2 = (bf16[64,18,1,1024]{3,0,2,1:T(8,128)(2,1)S(1)}, bf16[64,18,1,1024]{3,0,2,1:T(8,128)(2,1)}, u32[]{:S(2)}, u32[]{:S(2)}) collective-permute-start(bf16[64,18,1,1024]{3,0,2,1:T(8,128)(2,1)S(1)} %copy.50), channel_id=1, source_target_pairs={{0,4},{4,8},{8,12},{12,16},{16,20},{20,24},{24,28},{1,5},{5,9},{9,... | collective-permute-start | bytes 7077896 | tf_op jit(solution)/shard_map/ppermute | solution.py:12
  22.3 104.4 %collective-permute-start.1 = (bf16[64,18,1,1024]{3,0,2,1:T(8,128)(2,1)}, bf16[64,18,1,1024]{3,0,2,1:T(8,128)(2,1)}, u32[]{:S(2)}, u32[]{:S(2)}) collective-permute-start(bf16[64,18,1,1024]{3,0,2,1:T(8,128)(2,1)} %copy.49), channel_id=1, source_target_pairs={{4,0},{8,4},{12,8},{16,12},{20,16},{24,20},{28,24},{5,1},{9,5},{13... | collective-permute-start | bytes 7077896 | tf_op jit(solution)/shard_map/ppermute | solution.py:15
  27.3 14.0 %copy-start.1 = (bf16[18,2,1024]{2,1,0:T(2,128)(2,1)S(1)}, bf16[18,2,1024]{2,1,0:T(2,128)(2,1)}, u32[]{:S(2)}) copy-start(bf16[18,2,1024]{2,1,0:T(2,128)(2,1)} %param.10) | copy-start | bytes 221188
  197.7 58.8 %all-to-all-start = ((bf16[64,1,18,2,4,256]{5,3,2,0,1,4:T(2,128)(2,1)}), bf16[64,1,18,2,4,256]{5,3,2,0,1,4:T(2,128)(2,1)}, u32[]{:S(2)}, u32[]{:S(2)}) async-start(bf16[64,1,18,2,4,256]{5,3,2,0,1,4:T(2,128)(2,1)} %copy.38), calls=%async_computation | async-start | bytes 9437184 | tf_op jit(solution)/shard_map/all_to_all | solution.py:70
  202.9 11.6 %copy-start.2 = (bf16[72,512]{1,0:T(8,128)(2,1)S(1)}, bf16[72,512]{1,0:T(8,128)(2,1)}, u32[]{:S(2)}) copy-start(bf16[72,512]{1,0:T(8,128)(2,1)} %param.15) | copy-start | bytes 221188
  203.0 11.7 %copy-start.5 = (f32[64]{0:T(128)S(1)}, f32[64]{0:T(128)}, u32[]{:S(2)}) copy-start(f32[64]{0:T(128)} %param.16) | copy-start | bytes 772
  203.0 11.7 %copy-start.3 = (s32[512]{0:T(512)S(1)}, s32[512]{0:T(512)}, u32[]{:S(2)}) copy-start(s32[512]{0:T(512)} %param.13) | copy-start | bytes 6148
  256.5 10.9 %copy-start.4 = (s32[512]{0:T(512)S(1)}, s32[512]{0:T(512)}, u32[]{:S(2)}) copy-start(s32[512]{0:T(512)} %param.14) | copy-start | bytes 6148
  299.7 14.2 %copy-start.6 = (s32[16]{0:T(128)S(1)}, s32[16]{0:T(128)}, u32[]{:S(2)}) copy-start(s32[16]{0:T(128)} %param.17) | copy-start | bytes 196
  311.1 205.9 %collective-permute-start.3 = (bf16[64,72,512]{2,1,0:T(8,128)(2,1)}, bf16[64,72,512]{2,1,0:T(8,128)(2,1)}, u32[]{:S(2)}, u32[]{:S(2)}) collective-permute-start(bf16[64,72,512]{2,1,0:T(8,128)(2,1)} %copy.44), channel_id=1, source_target_pairs={{0,16},{4,20},{8,24},{12,28},{16,0},{20,4},{24,8},{28,12},{1,17},{... | collective-permute-start | bytes 14155784 | tf_op jit(solution)/shard_map/ppermute | solution.py:27
where the time goes:
time: 549 us; the launch traced here: 547 us
  waiting for transfers between devices  319 us (58%)
  local copies, waits for them, and re-layouts  131 us (24%)
  other arithmetic  56.8 us (10%)
  matrix products  21 us (4%)
  starting transfers between devices  17.8 us (3%)
    ppermute x1, waiting for transfers between devices, swapped(): lax.ppermute(shard, axis, [(i, i ^ 1 << apart) for i in range(lax.axis_si...  202 us
    ppermute x1, waiting for transfers between devices, padded_2(): lax.ppermute(lax.slice_in_dim(block, block.shape[dim] - width, None, axis...  75.8 us
    convert_element_type x1, other arithmetic, local(): advected = advect_block(center, south_side, north_side, south_face, north...  46.9 us
    all_to_all x1, waiting for transfers between devices, local(): lax.all_to_all(sectioned, 'lev', split_axis=4, concat_axis=1, tiled=True)  41.8 us
    unnamed x22, local copies, waits for them, and re-layouts  18.8 us
    dot_general x1, matrix products, convect(): jnp.einsum('kec,tec->tkc', matrix, tracers_bf, preferred_element_type=jnp...  16.7 us
    reshape x2, local copies, waits for them, and re-layouts, local(): advected.reshape(tracers, 1, lev_group, lat_dev, n_lev, lon_block)  16.7 us
    slice x2, local copies, waits for them, and re-layouts, advect_block(): jnp.roll(center, -1, axis=-1)  16.6 us
  transfers between devices with their start and end apart: 5, of which 3 were waited for; matrix products, arithmetic and copies ran while one was open for 10% of the time, Pallas kernels for 0%

commit v1 on v0

v1 whole, which is shorter than its diff:
```python
import functools

import jax
import jax.numpy as jnp
from jax import lax
from jax.experimental import pallas as pl
from jax.experimental.pallas import tpu as pltpu
from jax.sharding import PartitionSpec as P

UNIT = 8
STRIP = 16
LANES = 128
GROUP = 4


def shifted(value, axis, steps):
    count = lax.axis_size(axis)
    first, last = max(0, -steps), min(count, count - steps)
    return lax.ppermute(value, axis, [(i, i + steps) for i in range(first, last)])


def swapped(value, axis, apart):
    return lax.ppermute(value, axis, [(i, i ^ apart) for i in range(lax.axis_size(axis))])


def advect_kernel(n_lev, q0_ref, q1_ref, south_ref, north_ref, cs0_ref, cs1_ref, cn_ref, cw0_ref, cw1_ref, out_ref):
    f32 = jnp.float32
    rows, lon = q0_ref.shape
    block = lon // n_lev

    def lon_change(q, cw):
        west = cw * jnp.where(cw > 0, pltpu.roll(q, 1, 1), q)
        return pltpu.roll(west, lon - 1, 1) - west

    def strip(s, carry):
        at = pl.ds(pl.multiple_of(s * STRIP, STRIP), STRIP)
        q0, q1 = q0_ref[at, :].astype(f32), q1_ref[at, :].astype(f32)
        cs0, cs1, cn = (r[at, :].astype(f32) for r in (cs0_ref, cs1_ref, cn_ref))
        low = cs0 * jnp.where(cs0 > 0, south_ref[at, :].astype(f32), q0)
        mid = cs1 * jnp.where(cs1 > 0, q0, q1)
        high = cn * jnp.where(cn > 0, q1, north_ref[at, :].astype(f32))
        new0 = q0 - (mid - low) - lon_change(q0, cw0_ref[at, :].astype(f32))
        new1 = q1 - (high - mid) - lon_change(q1, cw1_ref[at, :].astype(f32))
        new0, new1 = new0.astype(out_ref.dtype), new1.astype(out_ref.dtype)
        for j in range(n_lev):
            out_ref[j, at, :block] = new0[:, j * block:(j + 1) * block]
            out_ref[j, at, block:] = new1[:, j * block:(j + 1) * block]
        return carry

    lax.fori_loop(0, rows // STRIP, strip, 0)


def advect(n_lev, q0, q1, south, north, faces):
    rows, lon = q0.shape
    unit = faces[0].shape[0]
    row_spec = pl.BlockSpec((unit, lon), lambda i: (i, 0))
    face_spec = pl.BlockSpec((unit, lon), lambda i: (0, 0))
    return pl.pallas_call(
        functools.partial(advect_kernel, n_lev),
        grid=(rows // unit,),
        in_specs=[row_spec] * 4 + [face_spec] * 5,
        out_specs=pl.BlockSpec((n_lev, unit, 2 * lon // n_lev), lambda i: (0, i, 0)),
        out_shape=jax.ShapeDtypeStruct((n_lev, rows, 2 * lon // n_lev), q0.dtype),
        compiler_params=pltpu.CompilerParams(vmem_limit_bytes=32 * 2**20),
        cost_estimate=pl.CostEstimate(flops=60 * rows * lon, bytes_accessed=12 * rows * lon, transcendentals=0),
        name="advect",
    )(q0, q1, south, north, *faces)


def physics_kernel(arrived_ref, placing_ref, matrix_ref, rain_ref, scav_ref, out_ref, x_ref):
    f32 = jnp.float32
    n_lev, rows, _ = arrived_ref.shape
    tracers, levels, lanes = out_ref.shape
    per = levels // n_lev
    for g in range(n_lev):
        x_ref[g] = jnp.dot(arrived_ref[g], placing_ref[...], preferred_element_type=f32)
    rain = rain_ref[...].astype(f32)

    def group(i, carry):
        t0 = i * GROUP
        sums = tuple(jnp.zeros((levels, lanes), f32) for _ in range(GROUP))
        for g in range(n_lev):
            def level(e, sums):
                m = matrix_ref[g * per + e].astype(f32)
                return tuple(
                    total + m * x_ref[g, pl.ds((t0 + u) * per + e, 1), :]
                    for u, total in enumerate(sums)
                )
            sums = lax.fori_loop(0, per, level, sums, unroll=2)
        for u in range(GROUP):
            out_ref[t0 + u] = (sums[u] * jnp.exp(-scav_ref[t0 + u] * rain)).astype(out_ref.dtype)
        return carry

    lax.fori_loop(0, tracers // GROUP, group, 0)


def physics(arrived, placing, matrix, rain, scav):
    n_lev, rows, columns = arrived.shape
    levels = rain.shape[0]
    tracers = scav.shape[0]
    return pl.pallas_call(
        physics_kernel,
        grid=(columns // LANES,),
        in_specs=[
            pl.BlockSpec(arrived.shape, lambda i: (0, 0, 0)),
            pl.BlockSpec((columns, LANES), lambda i: (0, i)),
            pl.BlockSpec((levels, levels, LANES), lambda i: (0, 0, i)),
            pl.BlockSpec((levels, LANES), lambda i: (0, i)),
            pl.BlockSpec(memory_space=pltpu.SMEM),
        ],
        out_specs=pl.BlockSpec((tracers, levels, LANES), lambda i: (0, 0, i)),
        out_shape=jax.ShapeDtypeStruct((tracers, levels, columns), arrived.dtype),
        scratch_shapes=[pltpu.VMEM((n_lev, rows, LANES), jnp.float32)],
        compiler_params=pltpu.CompilerParams(vmem_limit_bytes=40 * 2**20),
        cost_estimate=pl.CostEstimate(
            flops=40 * tracers * levels * levels * columns,
            bytes_accessed=4 * tracers * levels * columns + 2 * levels * levels * columns,
            transcendentals=tracers * levels * columns),
        name="physics",
    )(arrived, placing, matrix, rain, scav)


def chunks_of(tracers):
    units = tracers // UNIT
    parts, left, size = [], units, 1
    while left:
        take = min(size, left)
        parts.append(take * UNIT)
        left -= take
        if len(parts) >= 2:
            size = 2
    return parts


def local(tracer_dyn, courant_lat, courant_lon, conv_matrix, conv_mask, column_order, rain, scav_rate, pair_flag):
    n_lat = lax.axis_size("lat")
    n_lev = lax.axis_size("lev")
    tracers, per, _, lon = tracer_dyn.shape
    levels, _, columns = conv_matrix.shape

    def tiled(face):
        return jnp.tile(face, (UNIT, 1))

    faces = (
        tiled(courant_lat[:, 0]),
        tiled(courant_lat[:, 1]),
        tiled(shifted(courant_lat[:, 0], "lat", -1)),
        tiled(courant_lon[:, 0]),
        tiled(courant_lon[:, 1]),
    )
    parts = chunks_of(tracers)
    starts = [sum(parts[:c]) for c in range(len(parts))]
    rows = []
    for start, size in zip(starts, parts):
        piece = tracer_dyn[start:start + size]
        q0 = piece[:, :, 0].reshape(size * per, lon)
        q1 = piece[:, :, 1].reshape(size * per, lon)
        rows.append((q0, q1, shifted(q1, "lat", 1), shifted(q0, "lat", -1)))

    placing = (jnp.arange(columns, dtype=jnp.int32)[:, None] == column_order[None, :]).astype(jnp.bfloat16)
    keep = jnp.eye(levels, dtype=conv_matrix.dtype)[:, :, None]
    matrix = jnp.where(conv_mask[None, None, :] > 0, jnp.transpose(conv_matrix, (1, 0, 2)), keep)

    pair = lax.axis_index("lat") % (n_lat // 2) * n_lev + lax.axis_index("lev")
    trade = pair_flag[pair] > 0
    result = jnp.zeros((tracers, levels, columns), tracer_dyn.dtype)
    for c, (start, size) in enumerate(zip(starts, parts)):
        advected = advect(n_lev, *rows[c], faces)
        arrived = lax.all_to_all(advected, "lev", split_axis=0, concat_axis=0, tiled=True)
        washed = physics(arrived, placing, matrix, rain, scav_rate[start:start + size])
        partner = swapped(washed, "lat", n_lat // 2)
        chosen = jnp.where(trade, partner, washed)
        result = lax.dynamic_update_slice(result, chosen, (start, 0, 0))
    return result


def solution(mesh):
    placed = (
        P(None, "lev", "lat", None),
        P("lev", "lat", None),
        P("lev", "lat", None),
        P(None, None, ("lat", "lev")),
        P(("lat", "lev")),
        P(("lat", "lev")),
        P(None, ("lat", "lev")),
        P(),
        P(),
    )
    return jax.shard_map(
        local, mesh=mesh, in_specs=placed, out_specs=P(None, None, ("lat", "lev")), check_vma=False
    )
```

time: 549 us -> 415 us (0.76)
  waiting for transfers between devices: 319 us -> 169 us
  Pallas kernels: 0 us -> 112 us
  local copies, waits for them, and re-layouts: 131 us -> 50.6 us
  starting transfers between devices: 17.8 us -> 66.7 us
  other arithmetic: 56.8 us -> 14.6 us
  matrix products: 21 us -> 0 us
    pallas_call x0 -> x10, Pallas kernels: none -> 112 us  [the longest x5 92.1 us: physics(): pl.pallas_call(physics_kernel, grid=(columns // LANES,), in_specs=[pl.Blo...]
    ppermute x4 -> x16, waiting for transfers between devices: 278 us -> 167 us  [the longest x5 120 us: swapped(): lax.ppermute(value, axis, [(i, i ^ apart) for i in range(lax.axis_size(ax...]
    convert_element_type x4 -> x2, other arithmetic: 47.1 us -> 0.15 us  [the longest x1 0.14 us: local(): (jnp.arange(columns, dtype=jnp.int32)[:, None] == column_order[None, :])....]
    all_to_all x1 -> x5, waiting for transfers between devices: 41.8 us -> 1.52 us  [local(): lax.all_to_all(advected, 'lev', split_axis=0, concat_axis=0, tiled=True)]
    ppermute x4 -> x16, starting transfers between devices: 12.6 us -> 46.7 us  [the longest x11 37.5 us: shifted(): lax.ppermute(value, axis, [(i, i + steps) for i in range(first, last)])]
    reshape x3 -> x0, local copies, waits for them, and re-layouts: 27.8 us -> none  [the longest x2 16.7 us: local(): advected.reshape(tracers, 1, lev_group, lat_dev, n_lev, lon_block)]
    ppermute x3 -> x0, local copies, waits for them, and re-layouts: 26.2 us -> none  [the longest x1 11.2 us: swapped(): lax.ppermute(shard, axis, [(i, i ^ 1 << apart) for i in range(lax.axis_si...]
    dot_general x2 -> x0, matrix products: 21 us -> none  [the longest x1 16.7 us: convect(): jnp.einsum('kec,tec->tkc', matrix, tracers_bf, preferred_element_type=jnp...]
  transfers between devices with their start and end apart: 5 -> 21, of which waited for: 3 -> 8; matrix products, arithmetic and copies ran while one was open for 10% -> 13% of each run, Pallas kernels for 0% -> 27%
where the time goes in v1:
time: 415 us; the launch traced here: 414 us
  waiting for transfers between devices  169 us (41%)
  Pallas kernels  112 us (27%)
  starting transfers between devices  66.7 us (16%)
  local copies, waits for them, and re-layouts  50.6 us (12%)
  other arithmetic  14.6 us (4%)
    ppermute x5, waiting for transfers between devices, swapped(): lax.ppermute(value, axis, [(i, i ^ apart) for i in range(lax.axis_size(ax...  120 us
    pallas_call x5, Pallas kernels, physics(): pl.pallas_call(physics_kernel, grid=(columns // LANES,), in_specs=[pl.Blo...  92.1 us
    ppermute x11, waiting for transfers between devices, shifted(): lax.ppermute(value, axis, [(i, i + steps) for i in range(first, last)])  46.6 us
    ppermute x11, starting transfers between devices, shifted(): lax.ppermute(value, axis, [(i, i + steps) for i in range(first, last)])  37.5 us
    slice x2, local copies, waits for them, and re-layouts, local(): q1 = piece[:, :, 1].reshape(size * per, lon)  26.4 us
    pallas_call x5, Pallas kernels, advect(): pl.pallas_call(functools.partial(advect_kernel, n_lev), grid=(rows // uni...  20.1 us
    all_to_all x5, starting transfers between devices, local(): lax.all_to_all(advected, 'lev', split_axis=0, concat_axis=0, tiled=True)  20 us
    ppermute x5, starting transfers between devices, swapped(): lax.ppermute(value, axis, [(i, i ^ apart) for i in range(lax.axis_size(ax...  9.23 us
  transfers between devices with their start and end apart: 21, of which 8 were waited for; matrix products, arithmetic and copies ran while one was open for 13% of the time, Pallas kernels for 27%

profile of v1, /device:TPU:0, one launch (start us, length us, event | category | flops | bytes accessed | tf_op | source)
XLA Modules:
  0.0 413.7 jit_solution(7700105661575253394)
XLA Ops:
  2.4 6.9 %slice_reduce_fusion.6 = (bf16[8,18,1024]{2,1,0:T(8,128)(2,1)S(1)}, bf16[8,18,1024]{2,1,0:T(8,128)(2,1)S(1)}, bf16[8,18,1024]{2,1,0:T(8,128)(2,1)S(1)}, bf16[8,18,1024]{2,1,0:T(8,128)(2,1)S(1)}) fusion(bf16[64,18,2,1024]{3,2,1,0:T(2,128)(2,1)} %param.9), kind=kLoop, calls=%fused_computation.13 | loop fusion | bytes 2359296 | tf_op jit(solution)/shard_map/slice | solution.py:157
  10.9 6.1 %collective-permute-start = (bf16[144,1024]{1,0:T(8,128)(2,1)S(1)}, bf16[144,1024]{1,0:T(8,128)(2,1)S(1)}, u32[]{:S(2)}, u32[]{:S(2)}) collective-permute-start(bf16[144,1024]{1,0:T(8,128)(2,1)S(1)} %reshape_squeeze.31.q1_ref), channel_id=1, source_target_pairs={{0,4},{4,8},{8,12},{12,16},{16,20},{20,24},{24,28},{1,5},{5,9},{9,... | collective-permute-start | bytes 884744 | tf_op jit(solution)/shard_map/ppermute | solution.py:19
  20.0 6.2 %collective-permute-start.4 = (bf16[144,1024]{1,0:T(8,128)(2,1)}, bf16[144,1024]{1,0:T(8,128)(2,1)}, u32[]{:S(2)}, u32[]{:S(2)}) collective-permute-start(bf16[144,1024]{1,0:T(8,128)(2,1)} %reshape_squeeze.33.q1_ref), channel_id=1, source_target_pairs={{0,4},{4,8},{8,12},{12,16},{16,20},{20,24},{24,28},{1,5},{5,9},{9,... | collective-permute-start | bytes 884744 | tf_op jit(solution)/shard_map/ppermute | solution.py:19
  27.1 7.8 %collective-permute-done.south_ref = bf16[144,1024]{1,0:T(8,128)(2,1)S(1)} collective-permute-done((bf16[144,1024]{1,0:T(8,128)(2,1)S(1)}, bf16[144,1024]{1,0:T(8,128)(2,1)S(1)}, u32[]{:S(2)}, u32[]{:S(2)}) %collective-permute-start) | collective-permute-done | bytes 294944 | tf_op jit(solution)/shard_map/ppermute | solution.py:19
  40.9 19.5 %slice_reduce_fusion = (bf16[16,18,1024]{2,1,0:T(8,128)(2,1)}, bf16[16,18,1024]{2,1,0:T(8,128)(2,1)}, bf16[16,18,1024]{2,1,0:T(8,128)(2,1)}, bf16[16,18,1024]{2,...) fusion(bf16[64,18,2,1024]{3,2,1,0:T(2,128)(2,1)} %param.9), kind=kLoop, calls=%fused_computation.2 | loop fusion | bytes 7077888 | tf_op jit(solution)/shard_map/slice | solution.py:157
  64.3 5.8 %collective-permute-start.7 = (bf16[288,1024]{1,0:T(8,128)(2,1)S(1)}, bf16[288,1024]{1,0:T(8,128)(2,1)}, u32[]{:S(2)}, u32[]{:S(2)}) collective-permute-start(bf16[288,1024]{1,0:T(8,128)(2,1)S(1)} %reshape_squeeze.35.q1_ref), channel_id=1, source_target_pairs={{0,4},{4,8},{8,12},{12,16},{16,20},{20,24},{24,28},{1,5},{5,9},{9,... | collective-permute-start | bytes 1769480 | tf_op jit(solution)/shard_map/ppermute | solution.py:19
  80.1 13.2 %collective-permute-done.7.south_ref = bf16[288,1024]{1,0:T(8,128)(2,1)} collective-permute-done((bf16[288,1024]{1,0:T(8,128)(2,1)S(1)}, bf16[288,1024]{1,0:T(8,128)(2,1)}, u32[]{:S(2)}, u32[]{:S(2)}) %collective-permute-start.7) | collective-permute-done | bytes 589856 | tf_op jit(solution)/shard_map/ppermute | solution.py:19
  93.3 4.5 %advect.7 = bf16[4,288,512]{2,1,0:T(8,128)(2,1)S(1)} custom-call(bf16[288,1024]{1,0:T(8,128)(2,1)S(1)} %reshape_squeeze.34.q0_ref, bf16[288,1024]{1,0:T(8,128)(2,1)S(1)} %reshape_squeeze.35.q1_ref, bf16[288,1024]{1,0:T(8,128)(2,1)} %collective-permute-done.7.south_ref, bf16[288,1024]{1,0:T(8,128)(2,1)} %collective-permute-done.8.north_ref, ...), custom_call_target="tpu_custom_call" | custom-call | flops 17694720 | bytes 3538944 | tf_op jit(solution)/shard_map/advect/pallas_call | solution.py:58
  108.0 6.1 %collective-permute-start.10 = (bf16[288,1024]{1,0:T(8,128)(2,1)}, bf16[288,1024]{1,0:T(8,128)(2,1)}, u32[]{:S(2)}, u32[]{:S(2)}) collective-permute-start(bf16[288,1024]{1,0:T(8,128)(2,1)} %reshape_squeeze.37.q1_ref), channel_id=1, source_target_pairs={{0,4},{4,8},{8,12},{12,16},{16,20},{20,24},{24,28},{1,5},{5,9},{9,... | collective-permute-start | bytes 1769480 | tf_op jit(solution)/shard_map/ppermute | solution.py:19
  119.7 5.4 %collective-permute-start.13 = (bf16[288,1024]{1,0:T(8,128)(2,1)}, bf16[288,1024]{1,0:T(8,128)(2,1)}, u32[]{:S(2)}, u32[]{:S(2)}) collective-permute-start(bf16[288,1024]{1,0:T(8,128)(2,1)} %reshape_squeeze.39.q1_ref), channel_id=1, source_target_pairs={{0,4},{4,8},{8,12},{12,16},{16,20},{20,24},{24,28},{1,5},{5,9},{9,... | collective-permute-start | bytes 1769480 | tf_op jit(solution)/shard_map/ppermute | solution.py:19
  125.3 23.5 %collective-permute-done.10.south_ref = bf16[288,1024]{1,0:T(8,128)(2,1)} collective-permute-done((bf16[288,1024]{1,0:T(8,128)(2,1)}, bf16[288,1024]{1,0:T(8,128)(2,1)}, u32[]{:S(2)}, u32[]{:S(2)}) %collective-permute-start.10) | collective-permute-done | bytes 589856 | tf_op jit(solution)/shard_map/ppermute | solution.py:19
  148.8 4.7 %advect.8 = bf16[4,288,512]{2,1,0:T(8,128)(2,1)S(1)} custom-call(bf16[288,1024]{1,0:T(8,128)(2,1)} %reshape_squeeze.36.q0_ref, bf16[288,1024]{1,0:T(8,128)(2,1)} %reshape_squeeze.37.q1_ref, bf16[288,1024]{1,0:T(8,128)(2,1)} %collective-permute-done.10.south_ref, bf16[288,1024]{1,0:T(8,128)(2,1)} %collective-permute-done.11.north_ref, ...), custom_call_target="tpu_custom_call" | custom-call | flops 17694720 | bytes 3538944 | tf_op jit(solution)/shard_map/advect/pallas_call | solution.py:58
  154.5 4.4 %all-to-all-start.3 = ((bf16[4,288,512]{2,1,0:T(8,128)(2,1)}), bf16[4,288,512]{2,1,0:T(8,128)(2,1)}, u32[]{:S(2)}, u32[]{:S(2)}) async-start(bf16[4,288,512]{2,1,0:T(8,128)(2,1)} %copy-done.4), calls=%async_computation.3 | async-start | bytes 2359296 | tf_op jit(solution)/shard_map/all_to_all | solution.py:169
  159.0 8.7 %bitcast_select_fusion.matrix_ref = bf16[72,72,512]{2,1,0:T(8,128)(2,1)} fusion(bf16[72,72,512]{2,1,0:T(8,128)(2,1)} %param.12, pred[512]{0:T(512)(128)(4,1)S(1)} %broadcast_compare_fusion, bf16[72,72]{1,0:T(8,128)(2,1)S(1)} %fusion.1), kind=kLoop, calls=%fused_computation | loop fusion | flops 2654208 | bytes 10627712 | tf_op jit(solution)/shard_map/jit(_where)/select_n | solution.py:162
  167.7 4.7 %advect.9 = bf16[4,288,512]{2,1,0:T(8,128)(2,1)S(1)} custom-call(bf16[288,1024]{1,0:T(8,128)(2,1)} %reshape_squeeze.38.q0_ref, bf16[288,1024]{1,0:T(8,128)(2,1)} %reshape_squeeze.39.q1_ref, bf16[288,1024]{1,0:T(8,128)(2,1)} %collective-permute-done.13.south_ref, bf16[288,1024]{1,0:T(8,128)(2,1)} %collective-permute-done.14.north_ref, ...), custom_call_target="tpu_custom_call" | custom-call | flops 17694720 | bytes 3538944 | tf_op jit(solution)/shard_map/advect/pallas_call | solution.py:58
  174.9 4.4 %all-to-all-start.4 = ((bf16[4,288,512]{2,1,0:T(8,128)(2,1)}), bf16[4,288,512]{2,1,0:T(8,128)(2,1)}, u32[]{:S(2)}, u32[]{:S(2)}) async-start(bf16[4,288,512]{2,1,0:T(8,128)(2,1)} %copy-done.2), calls=%async_computation.4 | async-start | bytes 2359296 | tf_op jit(solution)/shard_map/all_to_all | solution.py:169
  182.0 22.1 %physics.7 = bf16[16,72,512]{2,1,0:T(8,128)(2,1)} custom-call(bf16[4,288,512]{2,1,0:T(8,128)(2,1)S(1)} %all-to-all-done.2.arrived_ref, bf16[512,512]{1,0:T(8,128)(2,1)S(1)} %fusion.placing_ref, bf16[72,72,512]{2,1,0:T(8,128)(2,1)S(1)} %copy-done, bf16[72,512]{1,0:T(8,128)(2,1)S(1)} %copy-done.7, f32[16]{0:T(128)S(1)} %get-tuple-element.20.scav_ref), custom_call_target="tpu_custom_call" | custom-call | flops 1698693120 | bytes 7667712 | tf_op jit(solution)/shard_map/physics/pallas_call | solution.py:101
  207.4 11.8 %physics.5 = bf16[8,72,512]{2,1,0:T(8,128)(2,1)S(1)} custom-call(bf16[4,144,512]{2,1,0:T(8,128)(2,1)S(1)} %copy-done.6, bf16[512,512]{1,0:T(8,128)(2,1)S(1)} %fusion.placing_ref, bf16[72,72,512]{2,1,0:T(8,128)(2,1)S(1)} %bitcast.14, bf16[72,512]{1,0:T(8,128)(2,1)S(1)} %copy-done.7, f32[8]{0:T(128)S(1)} %get-tuple-element.23.scav_ref), custom_call_target="tpu_custom_call" | custom-call | flops 849346560 | bytes 6488064 | tf_op jit(solution)/shard_map/physics/pallas_call | solution.py:101
  219.3 22.4 %physics.8 = bf16[16,72,512]{2,1,0:T(8,128)(2,1)S(1)} custom-call(bf16[4,288,512]{2,1,0:T(8,128)(2,1)} %all-to-all-done.3.arrived_ref, bf16[512,512]{1,0:T(8,128)(2,1)S(1)} %fusion.placing_ref, bf16[72,72,512]{2,1,0:T(8,128)(2,1)S(1)} %bitcast.14, bf16[72,512]{1,0:T(8,128)(2,1)S(1)} %copy-done.7, f32[16]{0:T(128)S(1)} %get-tuple-element.21.scav_ref), custom_call_target="tpu_custom_call" | custom-call | flops 1698693120 | bytes 7667712 | tf_op jit(solution)/shard_map/physics/pallas_call | solution.py:101
  244.6 12.9 %physics.6 = bf16[8,72,512]{2,1,0:T(8,128)(2,1)} custom-call(bf16[4,144,512]{2,1,0:T(8,128)(2,1)} %all-to-all-done.1.arrived_ref, bf16[512,512]{1,0:T(8,128)(2,1)S(1)} %fusion.placing_ref, bf16[72,72,512]{2,1,0:T(8,128)(2,1)S(1)} %bitcast.14, bf16[72,512]{1,0:T(8,128)(2,1)S(1)} %copy-done.7, f32[8]{0:T(128)S(1)} %get-tuple-element.22.scav_ref), custom_call_target="tpu_custom_call" | custom-call | flops 849346560 | bytes 6488064 | tf_op jit(solution)/shard_map/physics/pallas_call | solution.py:101
  260.1 22.9 %physics.9 = bf16[16,72,512]{2,1,0:T(8,128)(2,1)} custom-call(bf16[4,288,512]{2,1,0:T(8,128)(2,1)} %all-to-all-done.4.arrived_ref, bf16[512,512]{1,0:T(8,128)(2,1)S(1)} %fusion.placing_ref, bf16[72,72,512]{2,1,0:T(8,128)(2,1)S(1)} %copy-done.1, bf16[72,512]{1,0:T(8,128)(2,1)S(1)} %copy-done.7, f32[16]{0:T(128)S(1)} %get-tuple-element.19.scav_ref), custom_call_target="tpu_custom_call" | custom-call | flops 1698693120 | bytes 7667712 | tf_op jit(solution)/shard_map/physics/pallas_call | solution.py:101
  287.1 61.1 %collective-permute-done.3 = bf16[8,72,512]{2,1,0:T(8,128)(2,1)} collective-permute-done((bf16[8,72,512]{2,1,0:T(8,128)(2,1)S(1)}, bf16[8,72,512]{2,1,0:T(8,128)(2,1)}, u32[]{:S(2)}, u32[]{:S(2)}) %collective-permute-start.3) | collective-permute-done | bytes 589856 | tf_op jit(solution)/shard_map/ppermute | solution.py:23
  348.6 37.5 %collective-permute-done.6 = bf16[8,72,512]{2,1,0:T(8,128)(2,1)} collective-permute-done((bf16[8,72,512]{2,1,0:T(8,128)(2,1)}, bf16[8,72,512]{2,1,0:T(8,128)(2,1)}, u32[]{:S(2)}, u32[]{:S(2)}) %collective-permute-start.6) | collective-permute-done | bytes 589856 | tf_op jit(solution)/shard_map/ppermute | solution.py:23
  389.4 21.7 %collective-permute-done.15 = bf16[16,72,512]{2,1,0:T(8,128)(2,1)S(1)} collective-permute-done((bf16[16,72,512]{2,1,0:T(8,128)(2,1)}, bf16[16,72,512]{2,1,0:T(8,128)(2,1)S(1)}, u32[]{:S(2)}, u32[]{:S(2)}) %collective-permute-start.15) | collective-permute-done | bytes 1179680 | tf_op jit(solution)/shard_map/ppermute | solution.py:23
  (101 shorter events, 68.3 us)
Async XLA Ops:
  1.1 25.8 %collective-permute-start.2 = (bf16[18,1024]{1,0:T(8,128)(2,1)S(1)}, bf16[18,1024]{1,0:T(8,128)(2,1)S(1)}, u32[]{:S(2)}, u32[]{:S(2)}) collective-permute-start(bf16[18,1024]{1,0:T(8,128)(2,1)S(1)} %bitcast.15), channel_id=1, source_target_pairs={{4,0},{8,4},{12,8},{16,12},{20,16},{24,20},{28,24},{5,1},{9,5},{13... | collective-permute-start | bytes 110600 | tf_op jit(solution)/shard_map/ppermute | solution.py:19
  9.4 17.6 %collective-permute-start.1 = (bf16[144,1024]{1,0:T(8,128)(2,1)S(1)}, bf16[144,1024]{1,0:T(8,128)(2,1)S(1)}, u32[]{:S(2)}, u32[]{:S(2)}) collective-permute-start(bf16[144,1024]{1,0:T(8,128)(2,1)S(1)} %reshape_squeeze.30.q0_ref), channel_id=1, source_target_pairs={{4,0},{8,4},{12,8},{16,12},{20,16},{24,20},{28,24},{5,1},{9,5},{13... | collective-permute-start | bytes 884744 | tf_op jit(solution)/shard_map/ppermute | solution.py:19
  10.9 24.0 %collective-permute-start = (bf16[144,1024]{1,0:T(8,128)(2,1)S(1)}, bf16[144,1024]{1,0:T(8,128)(2,1)S(1)}, u32[]{:S(2)}, u32[]{:S(2)}) collective-permute-start(bf16[144,1024]{1,0:T(8,128)(2,1)S(1)} %reshape_squeeze.31.q1_ref), channel_id=1, source_target_pairs={{0,4},{4,8},{8,12},{12,16},{16,20},{20,24},{24,28},{1,5},{5,9},{9,... | collective-permute-start | bytes 884744 | tf_op jit(solution)/shard_map/ppermute | solution.py:19
  17.9 52.3 %collective-permute-start.5 = (bf16[144,1024]{1,0:T(8,128)(2,1)}, bf16[144,1024]{1,0:T(8,128)(2,1)}, u32[]{:S(2)}, u32[]{:S(2)}) collective-permute-start(bf16[144,1024]{1,0:T(8,128)(2,1)} %reshape_squeeze.32.q0_ref), channel_id=1, source_target_pairs={{4,0},{8,4},{12,8},{16,12},{20,16},{24,20},{28,24},{5,1},{9,5},{13... | collective-permute-start | bytes 884744 | tf_op jit(solution)/shard_map/ppermute | solution.py:19
  20.0 50.2 %collective-permute-start.4 = (bf16[144,1024]{1,0:T(8,128)(2,1)}, bf16[144,1024]{1,0:T(8,128)(2,1)}, u32[]{:S(2)}, u32[]{:S(2)}) collective-permute-start(bf16[144,1024]{1,0:T(8,128)(2,1)} %reshape_squeeze.33.q1_ref), channel_id=1, source_target_pairs={{0,4},{4,8},{8,12},{12,16},{16,20},{20,24},{24,28},{1,5},{5,9},{9,... | collective-permute-start | bytes 884744 | tf_op jit(solution)/shard_map/ppermute | solution.py:19
  37.4 36.5 %all-to-all-start = ((bf16[4,144,512]{2,1,0:T(8,128)(2,1)}), bf16[4,144,512]{2,1,0:T(8,128)(2,1)S(1)}, u32[]{:S(2)}, u32[]{:S(2)}) async-start(bf16[4,144,512]{2,1,0:T(8,128)(2,1)} %advect.5), calls=%async_computation | async-start | bytes 1179648 | tf_op jit(solution)/shard_map/all_to_all | solution.py:169
  61.7 18.4 %collective-permute-start.8 = (bf16[288,1024]{1,0:T(8,128)(2,1)S(1)}, bf16[288,1024]{1,0:T(8,128)(2,1)}, u32[]{:S(2)}, u32[]{:S(2)}) collective-permute-start(bf16[288,1024]{1,0:T(8,128)(2,1)S(1)} %reshape_squeeze.34.q0_ref), channel_id=1, source_target_pairs={{4,0},{8,4},{12,8},{16,12},{20,16},{24,20},{28,24},{5,1},{9,5},{13... | collective-permute-start | bytes 1769480 | tf_op jit(solution)/shard_map/ppermute | solution.py:19
  64.3 29.0 %collective-permute-start.7 = (bf16[288,1024]{1,0:T(8,128)(2,1)S(1)}, bf16[288,1024]{1,0:T(8,128)(2,1)}, u32[]{:S(2)}, u32[]{:S(2)}) collective-permute-start(bf16[288,1024]{1,0:T(8,128)(2,1)S(1)} %reshape_squeeze.35.q1_ref), channel_id=1, source_target_pairs={{0,4},{4,8},{8,12},{12,16},{16,20},{20,24},{24,28},{1,5},{5,9},{9,... | collective-permute-start | bytes 1769480 | tf_op jit(solution)/shard_map/ppermute | solution.py:19
  73.9 25.0 %all-to-all-start.1 = ((bf16[4,144,512]{2,1,0:T(8,128)(2,1)}), bf16[4,144,512]{2,1,0:T(8,128)(2,1)}, u32[]{:S(2)}, u32[]{:S(2)}) async-start(bf16[4,144,512]{2,1,0:T(8,128)(2,1)} %advect.6), calls=%async_computation.1 | async-start | bytes 1179648 | tf_op jit(solution)/shard_map/all_to_all | solution.py:169
  98.9 55.7 %all-to-all-start.2 = ((bf16[4,288,512]{2,1,0:T(8,128)(2,1)}), bf16[4,288,512]{2,1,0:T(8,128)(2,1)S(1)}, u32[]{:S(2)}, u32[]{:S(2)}) async-start(bf16[4,288,512]{2,1,0:T(8,128)(2,1)} %copy-done.3), calls=%async_computation.2 | async-start | bytes 2359296 | tf_op jit(solution)/shard_map/all_to_all | solution.py:169
  104.6 20.7 %collective-permute-start.11 = (bf16[288,1024]{1,0:T(8,128)(2,1)}, bf16[288,1024]{1,0:T(8,128)(2,1)}, u32[]{:S(2)}, u32[]{:S(2)}) collective-permute-start(bf16[288,1024]{1,0:T(8,128)(2,1)} %reshape_squeeze.36.q0_ref), channel_id=1, source_target_pairs={{4,0},{8,4},{12,8},{16,12},{20,16},{24,20},{28,24},{5,1},{9,5},{13... | collective-permute-start | bytes 1769480 | tf_op jit(solution)/shard_map/ppermute | solution.py:19
  108.0 40.8 %collective-permute-start.10 = (bf16[288,1024]{1,0:T(8,128)(2,1)}, bf16[288,1024]{1,0:T(8,128)(2,1)}, u32[]{:S(2)}, u32[]{:S(2)}) collective-permute-start(bf16[288,1024]{1,0:T(8,128)(2,1)} %reshape_squeeze.37.q1_ref), channel_id=1, source_target_pairs={{0,4},{4,8},{8,12},{12,16},{16,20},{20,24},{24,28},{1,5},{5,9},{9,... | collective-permute-start | bytes 1769480 | tf_op jit(solution)/shard_map/ppermute | solution.py:19
  116.3 51.4 %collective-permute-start.14 = (bf16[288,1024]{1,0:T(8,128)(2,1)}, bf16[288,1024]{1,0:T(8,128)(2,1)}, u32[]{:S(2)}, u32[]{:S(2)}) collective-permute-start(bf16[288,1024]{1,0:T(8,128)(2,1)} %reshape_squeeze.38.q0_ref), channel_id=1, source_target_pairs={{4,0},{8,4},{12,8},{16,12},{20,16},{24,20},{28,24},{5,1},{9,5},{13... | collective-permute-start | bytes 1769480 | tf_op jit(solution)/shard_map/ppermute | solution.py:19
  119.7 47.9 %collective-permute-start.13 = (bf16[288,1024]{1,0:T(8,128)(2,1)}, bf16[288,1024]{1,0:T(8,128)(2,1)}, u32[]{:S(2)}, u32[]{:S(2)}) collective-permute-start(bf16[288,1024]{1,0:T(8,128)(2,1)} %reshape_squeeze.39.q1_ref), channel_id=1, source_target_pairs={{0,4},{4,8},{8,12},{12,16},{16,20},{20,24},{24,28},{1,5},{5,9},{9,... | collective-permute-start | bytes 1769480 | tf_op jit(solution)/shard_map/ppermute | solution.py:19
  154.5 20.3 %all-to-all-start.3 = ((bf16[4,288,512]{2,1,0:T(8,128)(2,1)}), bf16[4,288,512]{2,1,0:T(8,128)(2,1)}, u32[]{:S(2)}, u32[]{:S(2)}) async-start(bf16[4,288,512]{2,1,0:T(8,128)(2,1)} %copy-done.4), calls=%async_computation.3 | async-start | bytes 2359296 | tf_op jit(solution)/shard_map/all_to_all | solution.py:169
  174.9 32.5 %slice-start = ((s8[5308416]{0:T(1024)(128)(4,1)}), s8[1114112]{0:T(1024)(128)(4,1)S(1)}, s32[]{:S(2)}) async-start(s8[5308416]{0:T(1024)(128)(4,1)} %bitcast.13), calls=%async_computation.5 | async-start | bytes 2228224
  174.9 82.7 %all-to-all-start.4 = ((bf16[4,288,512]{2,1,0:T(8,128)(2,1)}), bf16[4,288,512]{2,1,0:T(8,128)(2,1)}, u32[]{:S(2)}, u32[]{:S(2)}) async-start(bf16[4,288,512]{2,1,0:T(8,128)(2,1)} %copy-done.2), calls=%async_computation.4 | async-start | bytes 2359296 | tf_op jit(solution)/shard_map/all_to_all | solution.py:169
  182.0 25.4 %copy-start.6 = (bf16[4,144,512]{2,1,0:T(8,128)(2,1)S(1)}, bf16[4,144,512]{2,1,0:T(8,128)(2,1)}, u32[]{:S(2)}) copy-start(bf16[4,144,512]{2,1,0:T(8,128)(2,1)} %copy-done.5) | copy-start | bytes 1769476
  204.1 183.3 %collective-permute-start.9 = (bf16[16,72,512]{2,1,0:T(8,128)(2,1)}, bf16[16,72,512]{2,1,0:T(8,128)(2,1)}, u32[]{:S(2)}, u32[]{:S(2)}) collective-permute-start(bf16[16,72,512]{2,1,0:T(8,128)(2,1)} %physics.7), channel_id=1, source_target_pairs={{0,16},{4,20},{8,24},{12,28},{16,0},{20,4},{24,8},{28,12},{1,17},{... | collective-permute-start | bytes 3538952 | tf_op jit(solution)/shard_map/ppermute | solution.py:23
  219.2 129.1 %collective-permute-start.3 = (bf16[8,72,512]{2,1,0:T(8,128)(2,1)S(1)}, bf16[8,72,512]{2,1,0:T(8,128)(2,1)}, u32[]{:S(2)}, u32[]{:S(2)}) collective-permute-start(bf16[8,72,512]{2,1,0:T(8,128)(2,1)S(1)} %physics.5), channel_id=1, source_target_pairs={{0,16},{4,20},{8,24},{12,28},{16,0},{20,4},{24,8},{28,12},{1,17},{... | collective-permute-start | bytes 1769480 | tf_op jit(solution)/shard_map/ppermute | solution.py:23
  241.7 147.3 %collective-permute-start.12 = (bf16[16,72,512]{2,1,0:T(8,128)(2,1)S(1)}, bf16[16,72,512]{2,1,0:T(8,128)(2,1)}, u32[]{:S(2)}, u32[]{:S(2)}) collective-permute-start(bf16[16,72,512]{2,1,0:T(8,128)(2,1)S(1)} %physics.8), channel_id=1, source_target_pairs={{0,16},{4,20},{8,24},{12,28},{16,0},{20,4},{24,8},{28,12},{1,17},{... | collective-permute-start | bytes 3538952 | tf_op jit(solution)/shard_map/ppermute | solution.py:23
  257.5 128.6 %collective-permute-start.6 = (bf16[8,72,512]{2,1,0:T(8,128)(2,1)}, bf16[8,72,512]{2,1,0:T(8,128)(2,1)}, u32[]{:S(2)}, u32[]{:S(2)}) collective-permute-start(bf16[8,72,512]{2,1,0:T(8,128)(2,1)} %physics.6), channel_id=1, source_target_pairs={{0,16},{4,20},{8,24},{12,28},{16,0},{20,4},{24,8},{28,12},{1,17},{... | collective-permute-start | bytes 1769480 | tf_op jit(solution)/shard_map/ppermute | solution.py:23
  260.1 25.8 %copy-start.13 = (s32[16]{0:T(128)S(1)}, s32[16]{0:T(128)}, u32[]{:S(2)}) copy-start(s32[16]{0:T(128)} %param.17) | copy-start | bytes 196
  283.0 128.1 %collective-permute-start.15 = (bf16[16,72,512]{2,1,0:T(8,128)(2,1)}, bf16[16,72,512]{2,1,0:T(8,128)(2,1)S(1)}, u32[]{:S(2)}, u32[]{:S(2)}) collective-permute-start(bf16[16,72,512]{2,1,0:T(8,128)(2,1)} %physics.9), channel_id=1, source_target_pairs={{0,16},{4,20},{8,24},{12,28},{16,0},{20,4},{24,8},{28,12},{1,17},{... | collective-permute-start | bytes 3538952 | tf_op jit(solution)/shard_map/ppermute | solution.py:23
  (13 other events, 123.4 us)

commit v2 on v1

--- a/solution.py
+++ b/solution.py
@@ -23,7 +23,33 @@
     return lax.ppermute(value, axis, [(i, i ^ apart) for i in range(lax.axis_size(axis))])
 
 
-def advect_kernel(n_lev, q0_ref, q1_ref, south_ref, north_ref, cs0_ref, cs1_ref, cn_ref, cw0_ref, cw1_ref, out_ref):
+def split_kernel(q_ref, after_ref, q0_ref, q1_ref):
+    del after_ref
+    rows = q0_ref.shape[0]
+    row = lax.broadcasted_iota(jnp.int32, (rows, 2 * rows), 0)
+    column = lax.broadcasted_iota(jnp.int32, (rows, 2 * rows), 1)
+    for a, ref in enumerate((q0_ref, q1_ref)):
+        pick = (column == 2 * row + a).astype(jnp.float32).astype(q_ref.dtype)
+        ref[...] = jnp.dot(pick, q_ref[...], preferred_element_type=jnp.float32).astype(ref.dtype)
+
+
+def split(q, unit, after):
+    rows, lon = q.shape
+    half = jax.ShapeDtypeStruct((rows // 2, lon), q.dtype)
+    return pl.pallas_call(
+        split_kernel,
+        grid=(rows // 2 // unit,),
+        in_specs=[pl.BlockSpec((2 * unit, lon), lambda i: (i, 0)), pl.BlockSpec(memory_space=pl.ANY)],
+        out_specs=[pl.BlockSpec((unit, lon), lambda i: (i, 0))] * 2,
+        out_shape=[half, half],
+        compiler_params=pltpu.CompilerParams(vmem_limit_bytes=32 * 2**20),
+        cost_estimate=pl.CostEstimate(flops=4 * rows * lon, bytes_accessed=4 * rows * lon, transcendentals=0),
+        name="split",
+    )(q, after)
+
+
+def advect_kernel(n_lev, q0_ref, q1_ref, south_ref, north_ref, cs0_ref, cs1_ref, cn_ref, cw0_ref, cw1_ref, after_ref, out_ref):
+    del after_ref
     f32 = jnp.float32
     rows, lon = q0_ref.shape
     block = lon // n_lev
@@ -50,7 +76,7 @@
     lax.fori_loop(0, rows // STRIP, strip, 0)
 
 
-def advect(n_lev, q0, q1, south, north, faces):
+def advect(n_lev, q0, q1, south, north, faces, after):
     rows, lon = q0.shape
     unit = faces[0].shape[0]
     row_spec = pl.BlockSpec((unit, lon), lambda i: (i, 0))
@@ -58,13 +84,13 @@
     return pl.pallas_call(
         functools.partial(advect_kernel, n_lev),
         grid=(rows // unit,),
-        in_specs=[row_spec] * 4 + [face_spec] * 5,
+        in_specs=[row_spec] * 4 + [face_spec] * 5 + [pl.BlockSpec(memory_space=pl.ANY)],
         out_specs=pl.BlockSpec((n_lev, unit, 2 * lon // n_lev), lambda i: (0, i, 0)),
         out_shape=jax.ShapeDtypeStruct((n_lev, rows, 2 * lon // n_lev), q0.dtype),
         compiler_params=pltpu.CompilerParams(vmem_limit_bytes=32 * 2**20),
         cost_estimate=pl.CostEstimate(flops=60 * rows * lon, bytes_accessed=12 * rows * lon, transcendentals=0),
         name="advect",
-    )(q0, q1, south, north, *faces)
+    )(q0, q1, south, north, *faces, after)
 
 
 def physics_kernel(arrived_ref, placing_ref, matrix_ref, rain_ref, scav_ref, out_ref, x_ref):
@@ -86,7 +112,7 @@
                     total + m * x_ref[g, pl.ds((t0 + u) * per + e, 1), :]
                     for u, total in enumerate(sums)
                 )
-            sums = lax.fori_loop(0, per, level, sums, unroll=2)
+            sums = lax.fori_loop(0, per, level, sums, unroll=True)
         for u in range(GROUP):
             out_ref[t0 + u] = (sums[u] * jnp.exp(-scav_ref[t0 + u] * rain)).astype(out_ref.dtype)
         return carry
@@ -150,13 +176,6 @@
     )
     parts = chunks_of(tracers)
     starts = [sum(parts[:c]) for c in range(len(parts))]
-    rows = []
-    for start, size in zip(starts, parts):
-        piece = tracer_dyn[start:start + size]
-        q0 = piece[:, :, 0].reshape(size * per, lon)
-        q1 = piece[:, :, 1].reshape(size * per, lon)
-        rows.append((q0, q1, shifted(q1, "lat", 1), shifted(q0, "lat", -1)))
-
     placing = (jnp.arange(columns, dtype=jnp.int32)[:, None] == column_order[None, :]).astype(jnp.bfloat16)
     keep = jnp.eye(levels, dtype=conv_matrix.dtype)[:, :, None]
     matrix = jnp.where(conv_mask[None, None, :] > 0, jnp.transpose(conv_matrix, (1, 0, 2)), keep)
@@ -164,8 +183,17 @@
     pair = lax.axis_index("lat") % (n_lat // 2) * n_lev + lax.axis_index("lev")
     trade = pair_flag[pair] > 0
     result = jnp.zeros((tracers, levels, columns), tracer_dyn.dtype)
+    def sent(c, after):
+        piece = tracer_dyn[starts[c]:starts[c] + parts[c]].reshape(2 * parts[c] * per, lon)
+        q0, q1 = split(piece, UNIT * per, after)
+        return q0, q1, shifted(q1, "lat", 1), shifted(q0, "lat", -1)
+
+    ahead = [sent(0, faces[0]), sent(1, faces[1])]
+    washed = placing
     for c, (start, size) in enumerate(zip(starts, parts)):
-        advected = advect(n_lev, *rows[c], faces)
+        advected = advect(n_lev, *ahead[c], faces, washed)
+        if c + 2 < len(parts):
+            ahead.append(sent(c + 2, advected))
         arrived = lax.all_to_all(advected, "lev", split_axis=0, concat_axis=0, tiled=True)
         washed = physics(arrived, placing, matrix, rain, scav_rate[start:start + size])
         partner = swapped(washed, "lat", n_lat // 2)

time: 415 us -> 424 us (1.022)
  blocking collectives: 0 us -> 12.6 us
  waiting for transfers between devices: 169 us -> 175 us
  starting transfers between devices: 66.7 us -> 61.7 us
    ppermute x11, waiting for transfers between devices: 46.6 us -> 4.16 us  [shifted(): lax.ppermute(value, axis, [(i, i + steps) for i in range(first, last)])]
    ppermute x5, waiting for transfers between devices: 120 us -> 158 us  [swapped(): lax.ppermute(value, axis, [(i, i ^ apart) for i in range(lax.axis_size(ax...]
    slice x2, local copies, waits for them, and re-layouts: 26.4 us -> 6.95 us  [sent(): tracer_dyn[starts[c]:starts[c] + parts[c]].reshape(2 * parts[c] * per, lon)]
    unnamed x34 -> x62, local copies, waits for them, and re-layouts: 8.13 us -> 21.8 us
    another operation x10 -> x0, local copies, waits for them, and re-layouts: 13.1 us -> none  [the longest x5 6.59 us: local(): q0 = piece[:, :, 0].reshape(size * per, lon)]
    all_to_all x0 -> x1, blocking collectives: none -> 12.6 us  [local(): lax.all_to_all(advected, 'lev', split_axis=0, concat_axis=0, tiled=True)]
    all_to_all x5 -> x4, waiting for transfers between devices: 1.52 us -> 13.4 us  [local(): lax.all_to_all(advected, 'lev', split_axis=0, concat_axis=0, tiled=True)]
    reshape x0 -> x5, local copies, waits for them, and re-layouts: none -> 11.8 us  [sent(): tracer_dyn[starts[c]:starts[c] + parts[c]].reshape(2 * parts[c] * per, lon)]
  transfers between devices with their start and end apart: 21 -> 20, of which waited for: 8 -> 8; matrix products, arithmetic and copies ran while one was open for 13% -> 9% of each run, Pallas kernels for 27% -> 22%
where the time goes in v2:
time: 424 us; the launch traced here: 422 us
  waiting for transfers between devices  175 us (41%)
  Pallas kernels  108 us (25%)
  starting transfers between devices  61.7 us (15%)
  local copies, waits for them, and re-layouts  46.9 us (11%)
  other arithmetic  17.1 us (4%)
  blocking collectives  12.6 us (3%)
    ppermute x5, waiting for transfers between devices, swapped(): lax.ppermute(value, axis, [(i, i ^ apart) for i in range(lax.axis_size(ax...  158 us
    pallas_call x5, Pallas kernels, physics(): pl.pallas_call(physics_kernel, grid=(columns // LANES,), in_specs=[pl.Blo...  81.5 us
    ppermute x11, starting transfers between devices, shifted(): lax.ppermute(value, axis, [(i, i + steps) for i in range(first, last)])  36 us
    unnamed x62, local copies, waits for them, and re-layouts  21.8 us
    pallas_call x5, Pallas kernels, advect(): pl.pallas_call(functools.partial(advect_kernel, n_lev), grid=(rows // uni...  19.5 us
    all_to_all x4, starting transfers between devices, local(): lax.all_to_all(advected, 'lev', split_axis=0, concat_axis=0, tiled=True)  17.3 us
    all_to_all x4, waiting for transfers between devices, local(): lax.all_to_all(advected, 'lev', split_axis=0, concat_axis=0, tiled=True)  13.4 us
    all_to_all x1, blocking collectives, local(): lax.all_to_all(advected, 'lev', split_axis=0, concat_axis=0, tiled=True)  12.6 us
  transfers between devices with their start and end apart: 20, of which 8 were waited for; matrix products, arithmetic and copies ran while one was open for 9% of the time, Pallas kernels for 22%

profile of v2, /device:TPU:0, one launch (start us, length us, event | category | flops | bytes accessed | tf_op | source)
XLA Modules:
  0.0 422.5 jit_solution(7490519561084906413)
XLA Ops:
  7.3 6.8 %collective-permute-start.4 = (bf16[144,1024]{1,0:T(8,128)(2,1)}, bf16[144,1024]{1,0:T(8,128)(2,1)}, u32[]{:S(2)}, u32[]{:S(2)}) collective-permute-start(bf16[144,1024]{1,0:T(8,128)(2,1)} %get-tuple-element.18.q1_ref), channel_id=1, source_target_pairs={{0,4},{4,8},{8,12},{12,16},{16,20},{20,24},{24,28},{1,5},{5,9},{9,... | collective-permute-start | bytes 884744 | tf_op jit(solution)/shard_map/ppermute | solution.py:19
  16.3 4.8 %collective-permute-start = (bf16[144,1024]{1,0:T(8,128)(2,1)S(1)}, bf16[144,1024]{1,0:T(8,128)(2,1)S(1)}, u32[]{:S(2)}, u32[]{:S(2)}) collective-permute-start(bf16[144,1024]{1,0:T(8,128)(2,1)S(1)} %get-tuple-element.16.q1_ref), channel_id=1, source_target_pairs={{0,4},{4,8},{8,12},{12,16},{16,20},{20,24},{24,28},{1,5},{5,9},{9,... | collective-permute-start | bytes 884744 | tf_op jit(solution)/shard_map/ppermute | solution.py:19
  21.3 8.7 %bitcast_select_fusion.matrix_ref = bf16[72,72,512]{2,1,0:T(8,128)(2,1)} fusion(bf16[72,72,512]{2,1,0:T(8,128)(2,1)} %param.12, pred[512]{0:T(512)(128)(4,1)S(1)} %broadcast_compare_fusion, bf16[72,72]{1,0:T(8,128)(2,1)S(1)} %fusion.1), kind=kLoop, calls=%fused_computation | loop fusion | flops 2654208 | bytes 10627712 | tf_op jit(solution)/shard_map/jit(_where)/select_n | solution.py:181
  40.4 4.2 all-to-all-start
  44.5 4.9 %fusion.2 = (bf16[16,18,2,1024]{3,2,1,0:T(2,128)(2,1)}, bf16[16,18,2,1024]{3,2,1,0:T(2,128)(2,1)}, bf16[16,18,2,1024]{3,2,1,0:T(2,128)(2,1)}) fusion(bf16[64,18,2,1024]{3,2,1,0:T(2,128)(2,1)} %param.9), kind=kLoop, calls=%fused_computation.15 | loop fusion | bytes 7077888 | tf_op jit(solution)/shard_map/slice | solution.py:187
  57.6 5.9 %collective-permute-start.7 = (bf16[288,1024]{1,0:T(8,128)(2,1)}, bf16[288,1024]{1,0:T(8,128)(2,1)}, u32[]{:S(2)}, u32[]{:S(2)}) collective-permute-start(bf16[288,1024]{1,0:T(8,128)(2,1)} %get-tuple-element.20.q1_ref), channel_id=1, source_target_pairs={{0,4},{4,8},{8,12},{12,16},{16,20},{20,24},{24,28},{1,5},{5,9},{9,... | collective-permute-start | bytes 1769480 | tf_op jit(solution)/shard_map/ppermute | solution.py:19
  66.0 10.9 %physics.5.after_ref = bf16[8,72,512]{2,1,0:T(8,128)(2,1)S(1)} custom-call(bf16[4,144,512]{2,1,0:T(8,128)(2,1)} %all-to-all-done.arrived_ref, bf16[512,512]{1,0:T(8,128)(2,1)S(1)} %fusion.after_ref.placing_ref, bf16[72,72,512]{2,1,0:T(8,128)(2,1)S(1)} %copy-done, bf16[72,512]{1,0:T(8,128)(2,1)S(1)} %copy-done.21, f32[8]{0:T(128)S(1)} %get-tuple-element.38.scav_ref), custom_call_target="tpu_custom_call" | custom-call | flops 849346560 | bytes 6488064 | tf_op jit(solution)/shard_map/physics/pallas_call | solution.py:127
  80.1 12.6 %all_to_all.25.arrived_ref = bf16[4,144,512]{2,1,0:T(8,128)(2,1)S(1)} all-to-all(bf16[4,144,512]{2,1,0:T(8,128)(2,1)S(1)} %advect.6.after_ref), channel_id=1, replica_groups=mesh['lat'=8,'lev'=4] {'lev'}, dimensions={0} | all-to-all | bytes 1179648 | tf_op jit(solution)/shard_map/all_to_all | solution.py:197
  93.5 10.2 %physics.6.after_ref = bf16[8,72,512]{2,1,0:T(8,128)(2,1)S(1)} custom-call(bf16[4,144,512]{2,1,0:T(8,128)(2,1)S(1)} %all_to_all.25.arrived_ref, bf16[512,512]{1,0:T(8,128)(2,1)S(1)} %fusion.after_ref.placing_ref, bf16[72,72,512]{2,1,0:T(8,128)(2,1)S(1)} %bitcast.14, bf16[72,512]{1,0:T(8,128)(2,1)S(1)} %copy-done.21, f32[8]{0:T(128)S(1)} %get-tuple-element.37.scav_ref), custom_call_target="tpu_custom_call" | custom-call | flops 849346560 | bytes 6488064 | tf_op jit(solution)/shard_map/physics/pallas_call | solution.py:127
  103.8 4.7 %advect.7.after_ref = bf16[4,288,512]{2,1,0:T(8,128)(2,1)S(1)} custom-call(bf16[288,1024]{1,0:T(8,128)(2,1)} %get-tuple-element.19.q0_ref, bf16[288,1024]{1,0:T(8,128)(2,1)} %get-tuple-element.20.q1_ref, bf16[288,1024]{1,0:T(8,128)(2,1)} %collective-permute-done.7.south_ref, bf16[288,1024]{1,0:T(8,128)(2,1)} %collective-permute-done.8.north_ref, ...), custom_call_target="tpu_custom_call" | custom-call | flops 17694720 | bytes 3538944 | tf_op jit(solution)/shard_map/advect/pallas_call | solution.py:84
  110.5 4.3 %all-to-all-start.2 = ((bf16[4,288,512]{2,1,0:T(8,128)(2,1)}), bf16[4,288,512]{2,1,0:T(8,128)(2,1)}, u32[]{:S(2)}, u32[]{:S(2)}) async-start(bf16[4,288,512]{2,1,0:T(8,128)(2,1)} %copy-done.8), calls=%async_computation.2 | async-start | bytes 2359296 | tf_op jit(solution)/shard_map/all_to_all | solution.py:197
  122.8 5.4 %collective-permute-start.10 = (bf16[288,1024]{1,0:T(8,128)(2,1)}, bf16[288,1024]{1,0:T(8,128)(2,1)}, u32[]{:S(2)}, u32[]{:S(2)}) collective-permute-start(bf16[288,1024]{1,0:T(8,128)(2,1)} %get-tuple-element.22.q1_ref), channel_id=1, source_target_pairs={{0,4},{4,8},{8,12},{12,16},{16,20},{20,24},{24,28},{1,5},{5,9},{9,... | collective-permute-start | bytes 1769480 | tf_op jit(solution)/shard_map/ppermute | solution.py:19
  133.2 19.9 %physics.7.after_ref = bf16[16,72,512]{2,1,0:T(8,128)(2,1)S(1)} custom-call(bf16[4,288,512]{2,1,0:T(8,128)(2,1)} %all-to-all-done.2.arrived_ref, bf16[512,512]{1,0:T(8,128)(2,1)S(1)} %fusion.after_ref.placing_ref, bf16[72,72,512]{2,1,0:T(8,128)(2,1)S(1)} %copy-done.1, bf16[72,512]{1,0:T(8,128)(2,1)S(1)} %copy-done.21, f32[16]{0:T(128)S(1)} %get-tuple-element.35.scav_ref), custom_call_target="tpu_custom_call" | custom-call | flops 1698693120 | bytes 7667712 | tf_op jit(solution)/shard_map/physics/pallas_call | solution.py:127
  153.1 4.6 %advect.8 = bf16[4,288,512]{2,1,0:T(8,128)(2,1)S(1)} custom-call(bf16[288,1024]{1,0:T(8,128)(2,1)} %get-tuple-element.21.q0_ref, bf16[288,1024]{1,0:T(8,128)(2,1)} %get-tuple-element.22.q1_ref, bf16[288,1024]{1,0:T(8,128)(2,1)} %collective-permute-done.10.south_ref, bf16[288,1024]{1,0:T(8,128)(2,1)S(1)} %collective-permute-done.11.north_ref, ...), custom_call_target="tpu_custom_call" | custom-call | flops 17694720 | bytes 3538944 | tf_op jit(solution)/shard_map/advect/pallas_call | solution.py:84
  159.9 4.3 %all-to-all-start.3 = ((bf16[4,288,512]{2,1,0:T(8,128)(2,1)}), bf16[4,288,512]{2,1,0:T(8,128)(2,1)}, u32[]{:S(2)}, u32[]{:S(2)}) async-start(bf16[4,288,512]{2,1,0:T(8,128)(2,1)} %copy-done.20), calls=%async_computation.3 | async-start | bytes 2359296 | tf_op jit(solution)/shard_map/all_to_all | solution.py:197
  173.4 5.4 %collective-permute-start.13 = (bf16[288,1024]{1,0:T(8,128)(2,1)}, bf16[288,1024]{1,0:T(8,128)(2,1)}, u32[]{:S(2)}, u32[]{:S(2)}) collective-permute-start(bf16[288,1024]{1,0:T(8,128)(2,1)} %get-tuple-element.24.q1_ref), channel_id=1, source_target_pairs={{0,4},{4,8},{8,12},{12,16},{16,20},{20,24},{24,28},{1,5},{5,9},{9,... | collective-permute-start | bytes 1769480 | tf_op jit(solution)/shard_map/ppermute | solution.py:19
  182.6 19.9 %physics.8.after_ref = bf16[16,72,512]{2,1,0:T(8,128)(2,1)S(1)} custom-call(bf16[4,288,512]{2,1,0:T(8,128)(2,1)} %all-to-all-done.3.arrived_ref, bf16[512,512]{1,0:T(8,128)(2,1)S(1)} %fusion.after_ref.placing_ref, bf16[72,72,512]{2,1,0:T(8,128)(2,1)S(1)} %copy-done.2, bf16[72,512]{1,0:T(8,128)(2,1)S(1)} %copy-done.21, f32[16]{0:T(128)S(1)} %get-tuple-element.36.scav_ref), custom_call_target="tpu_custom_call" | custom-call | flops 1698693120 | bytes 7667712 | tf_op jit(solution)/shard_map/physics/pallas_call | solution.py:127
  203.5 4.6 %advect.9 = bf16[4,288,512]{2,1,0:T(8,128)(2,1)S(1)} custom-call(bf16[288,1024]{1,0:T(8,128)(2,1)S(1)} %get-tuple-element.23.q0_ref, bf16[288,1024]{1,0:T(8,128)(2,1)} %get-tuple-element.24.q1_ref, bf16[288,1024]{1,0:T(8,128)(2,1)} %collective-permute-done.13.south_ref, bf16[288,1024]{1,0:T(8,128)(2,1)} %collective-permute-done.14.north_ref, ...), custom_call_target="tpu_custom_call" | custom-call | flops 17694720 | bytes 3538944 | tf_op jit(solution)/shard_map/advect/pallas_call | solution.py:84
  209.2 4.6 %all-to-all-start.4 = ((bf16[4,288,512]{2,1,0:T(8,128)(2,1)}), bf16[4,288,512]{2,1,0:T(8,128)(2,1)}, u32[]{:S(2)}, u32[]{:S(2)}) async-start(bf16[4,288,512]{2,1,0:T(8,128)(2,1)} %copy-done.19), calls=%async_computation.4 | async-start | bytes 2359296 | tf_op jit(solution)/shard_map/all_to_all | solution.py:197
  219.7 9.8 %all-to-all-done.4.arrived_ref = bf16[4,288,512]{2,1,0:T(8,128)(2,1)} async-done(((bf16[4,288,512]{2,1,0:T(8,128)(2,1)}), bf16[4,288,512]{2,1,0:T(8,128)(2,1)}, u32[]{:S(2)}, u32[]{:S(2)}) %all-to-all-start.4) | async-done | bytes 1179680 | tf_op jit(solution)/shard_map/all_to_all | solution.py:197
  232.0 20.5 %physics.9 = bf16[16,72,512]{2,1,0:T(8,128)(2,1)} custom-call(bf16[4,288,512]{2,1,0:T(8,128)(2,1)} %all-to-all-done.4.arrived_ref, bf16[512,512]{1,0:T(8,128)(2,1)S(1)} %fusion.after_ref.placing_ref, bf16[72,72,512]{2,1,0:T(8,128)(2,1)S(1)} %copy-done.3, bf16[72,512]{1,0:T(8,128)(2,1)S(1)} %copy-done.21, f32[16]{0:T(128)S(1)} %get-tuple-element.34.scav_ref), custom_call_target="tpu_custom_call" | custom-call | flops 1698693120 | bytes 7667712 | tf_op jit(solution)/shard_map/physics/pallas_call | solution.py:127
  256.1 101.4 %collective-permute-done.3 = bf16[8,72,512]{2,1,0:T(8,128)(2,1)} collective-permute-done((bf16[8,72,512]{2,1,0:T(8,128)(2,1)S(1)}, bf16[8,72,512]{2,1,0:T(8,128)(2,1)}, u32[]{:S(2)}, u32[]{:S(2)}) %collective-permute-start.3) | collective-permute-done | bytes 589856 | tf_op jit(solution)/shard_map/ppermute | solution.py:23
  358.9 36.5 %collective-permute-done.6 = bf16[8,72,512]{2,1,0:T(8,128)(2,1)} collective-permute-done((bf16[8,72,512]{2,1,0:T(8,128)(2,1)S(1)}, bf16[8,72,512]{2,1,0:T(8,128)(2,1)}, u32[]{:S(2)}, u32[]{:S(2)}) %collective-permute-start.6) | collective-permute-done | bytes 589856 | tf_op jit(solution)/shard_map/ppermute | solution.py:23
  400.0 19.9 %collective-permute-done.15 = bf16[16,72,512]{2,1,0:T(8,128)(2,1)} collective-permute-done((bf16[16,72,512]{2,1,0:T(8,128)(2,1)}, bf16[16,72,512]{2,1,0:T(8,128)(2,1)}, u32[]{:S(2)}, u32[]{:S(2)}) %collective-permute-start.15) | collective-permute-done | bytes 1179680 | tf_op jit(solution)/shard_map/ppermute | solution.py:23
  (128 shorter events, 86.6 us)
Async XLA Ops:
  1.1 31.0 %collective-permute-start.2 = (bf16[18,1024]{1,0:T(8,128)(2,1)S(1)}, bf16[18,1024]{1,0:T(8,128)(2,1)S(1)}, u32[]{:S(2)}, u32[]{:S(2)}) collective-permute-start(bf16[18,1024]{1,0:T(8,128)(2,1)S(1)} %bitcast.15), channel_id=1, source_target_pairs={{4,0},{8,4},{12,8},{16,12},{20,16},{24,20},{28,24},{5,1},{9,5},{13... | collective-permute-start | bytes 110600 | tf_op jit(solution)/shard_map/ppermute | solution.py:19
  6.0 70.9 %collective-permute-start.5 = (bf16[144,1024]{1,0:T(8,128)(2,1)}, bf16[144,1024]{1,0:T(8,128)(2,1)}, u32[]{:S(2)}, u32[]{:S(2)}) collective-permute-start(bf16[144,1024]{1,0:T(8,128)(2,1)} %get-tuple-element.17.q0_ref), channel_id=1, source_target_pairs={{4,0},{8,4},{12,8},{16,12},{20,16},{24,20},{28,24},{5,1},{9,5},{13... | collective-permute-start | bytes 884744 | tf_op jit(solution)/shard_map/ppermute | solution.py:19
  7.3 69.7 %collective-permute-start.4 = (bf16[144,1024]{1,0:T(8,128)(2,1)}, bf16[144,1024]{1,0:T(8,128)(2,1)}, u32[]{:S(2)}, u32[]{:S(2)}) collective-permute-start(bf16[144,1024]{1,0:T(8,128)(2,1)} %get-tuple-element.18.q1_ref), channel_id=1, source_target_pairs={{0,4},{4,8},{8,12},{12,16},{16,20},{20,24},{24,28},{1,5},{5,9},{9,... | collective-permute-start | bytes 884744 | tf_op jit(solution)/shard_map/ppermute | solution.py:19
  15.0 19.0 %collective-permute-start.1 = (bf16[144,1024]{1,0:T(8,128)(2,1)S(1)}, bf16[144,1024]{1,0:T(8,128)(2,1)S(1)}, u32[]{:S(2)}, u32[]{:S(2)}) collective-permute-start(bf16[144,1024]{1,0:T(8,128)(2,1)S(1)} %get-tuple-element.15.q0_ref), channel_id=1, source_target_pairs={{4,0},{8,4},{12,8},{16,12},{20,16},{24,20},{28,24},{5,1},{9,5},{13... | collective-permute-start | bytes 884744 | tf_op jit(solution)/shard_map/ppermute | solution.py:19
  16.3 21.5 %collective-permute-start = (bf16[144,1024]{1,0:T(8,128)(2,1)S(1)}, bf16[144,1024]{1,0:T(8,128)(2,1)S(1)}, u32[]{:S(2)}, u32[]{:S(2)}) collective-permute-start(bf16[144,1024]{1,0:T(8,128)(2,1)S(1)} %get-tuple-element.16.q1_ref), channel_id=1, source_target_pairs={{0,4},{4,8},{8,12},{12,16},{16,20},{20,24},{24,28},{1,5},{5,9},{9,... | collective-permute-start | bytes 884744 | tf_op jit(solution)/shard_map/ppermute | solution.py:19
  40.4 23.2 %all-to-all-start = ((bf16[4,144,512]{2,1,0:T(8,128)(2,1)}), bf16[4,144,512]{2,1,0:T(8,128)(2,1)}, u32[]{:S(2)}, u32[]{:S(2)}) async-start(bf16[4,144,512]{2,1,0:T(8,128)(2,1)} %advect.5.after_ref), calls=%async_computation | async-start | bytes 1179648 | tf_op jit(solution)/shard_map/all_to_all | solution.py:197
  49.4 44.1 %slice-start = ((s8[5308416]{0:T(1024)(128)(4,1)}), s8[1114112]{0:T(1024)(128)(4,1)S(1)}, s32[]{:S(2)}) async-start(s8[5308416]{0:T(1024)(128)(4,1)} %bitcast.13), calls=%async_computation.5 | async-start | bytes 2228224
  56.3 47.4 %collective-permute-start.8 = (bf16[288,1024]{1,0:T(8,128)(2,1)}, bf16[288,1024]{1,0:T(8,128)(2,1)}, u32[]{:S(2)}, u32[]{:S(2)}) collective-permute-start(bf16[288,1024]{1,0:T(8,128)(2,1)} %get-tuple-element.19.q0_ref), channel_id=1, source_target_pairs={{4,0},{8,4},{12,8},{16,12},{20,16},{24,20},{28,24},{5,1},{9,5},{13... | collective-permute-start | bytes 1769480 | tf_op jit(solution)/shard_map/ppermute | solution.py:19
  57.6 46.2 %collective-permute-start.7 = (bf16[288,1024]{1,0:T(8,128)(2,1)}, bf16[288,1024]{1,0:T(8,128)(2,1)}, u32[]{:S(2)}, u32[]{:S(2)}) collective-permute-start(bf16[288,1024]{1,0:T(8,128)(2,1)} %get-tuple-element.20.q1_ref), channel_id=1, source_target_pairs={{0,4},{4,8},{8,12},{12,16},{16,20},{20,24},{24,28},{1,5},{5,9},{9,... | collective-permute-start | bytes 1769480 | tf_op jit(solution)/shard_map/ppermute | solution.py:19
  66.0 27.5 %slice-start.1 = ((s8[5308416]{0:T(1024)(128)(4,1)}), s8[4194304]{0:T(1024)(128)(4,1)S(1)}, s32[]{:S(2)}) async-start(s8[5308416]{0:T(1024)(128)(4,1)} %bitcast.13), calls=%async_computation.6 | async-start | bytes 8388608
  110.5 20.2 %all-to-all-start.2 = ((bf16[4,288,512]{2,1,0:T(8,128)(2,1)}), bf16[4,288,512]{2,1,0:T(8,128)(2,1)}, u32[]{:S(2)}, u32[]{:S(2)}) async-start(bf16[4,288,512]{2,1,0:T(8,128)(2,1)} %copy-done.8), calls=%async_computation.2 | async-start | bytes 2359296 | tf_op jit(solution)/shard_map/all_to_all | solution.py:197
  121.5 31.6 %collective-permute-start.11 = (bf16[288,1024]{1,0:T(8,128)(2,1)}, bf16[288,1024]{1,0:T(8,128)(2,1)S(1)}, u32[]{:S(2)}, u32[]{:S(2)}) collective-permute-start(bf16[288,1024]{1,0:T(8,128)(2,1)} %get-tuple-element.21.q0_ref), channel_id=1, source_target_pairs={{4,0},{8,4},{12,8},{16,12},{20,16},{24,20},{28,24},{5,1},{9,5},{13... | collective-permute-start | bytes 1769480 | tf_op jit(solution)/shard_map/ppermute | solution.py:19
  122.8 30.3 %collective-permute-start.10 = (bf16[288,1024]{1,0:T(8,128)(2,1)}, bf16[288,1024]{1,0:T(8,128)(2,1)}, u32[]{:S(2)}, u32[]{:S(2)}) collective-permute-start(bf16[288,1024]{1,0:T(8,128)(2,1)} %get-tuple-element.22.q1_ref), channel_id=1, source_target_pairs={{0,4},{4,8},{8,12},{12,16},{16,20},{20,24},{24,28},{1,5},{5,9},{9,... | collective-permute-start | bytes 1769480 | tf_op jit(solution)/shard_map/ppermute | solution.py:19
  159.9 20.2 %all-to-all-start.3 = ((bf16[4,288,512]{2,1,0:T(8,128)(2,1)}), bf16[4,288,512]{2,1,0:T(8,128)(2,1)}, u32[]{:S(2)}, u32[]{:S(2)}) async-start(bf16[4,288,512]{2,1,0:T(8,128)(2,1)} %copy-done.20), calls=%async_computation.3 | async-start | bytes 2359296 | tf_op jit(solution)/shard_map/all_to_all | solution.py:197
  172.1 30.4 %collective-permute-start.14 = (bf16[288,1024]{1,0:T(8,128)(2,1)S(1)}, bf16[288,1024]{1,0:T(8,128)(2,1)}, u32[]{:S(2)}, u32[]{:S(2)}) collective-permute-start(bf16[288,1024]{1,0:T(8,128)(2,1)S(1)} %get-tuple-element.23.q0_ref), channel_id=1, source_target_pairs={{4,0},{8,4},{12,8},{16,12},{20,16},{24,20},{28,24},{5,1},{9,5},{13... | collective-permute-start | bytes 1769480 | tf_op jit(solution)/shard_map/ppermute | solution.py:19
  173.4 29.5 %collective-permute-start.13 = (bf16[288,1024]{1,0:T(8,128)(2,1)}, bf16[288,1024]{1,0:T(8,128)(2,1)}, u32[]{:S(2)}, u32[]{:S(2)}) collective-permute-start(bf16[288,1024]{1,0:T(8,128)(2,1)} %get-tuple-element.24.q1_ref), channel_id=1, source_target_pairs={{0,4},{4,8},{8,12},{12,16},{16,20},{20,24},{24,28},{1,5},{5,9},{9,... | collective-permute-start | bytes 1769480 | tf_op jit(solution)/shard_map/ppermute | solution.py:19
  209.2 20.4 %all-to-all-start.4 = ((bf16[4,288,512]{2,1,0:T(8,128)(2,1)}), bf16[4,288,512]{2,1,0:T(8,128)(2,1)}, u32[]{:S(2)}, u32[]{:S(2)}) async-start(bf16[4,288,512]{2,1,0:T(8,128)(2,1)} %copy-done.19), calls=%async_computation.4 | async-start | bytes 2359296 | tf_op jit(solution)/shard_map/all_to_all | solution.py:197
  213.8 182.8 %collective-permute-start.9 = (bf16[16,72,512]{2,1,0:T(8,128)(2,1)S(1)}, bf16[16,72,512]{2,1,0:T(8,128)(2,1)}, u32[]{:S(2)}, u32[]{:S(2)}) collective-permute-start(bf16[16,72,512]{2,1,0:T(8,128)(2,1)S(1)} %copy-done.5), channel_id=1, source_target_pairs={{0,16},{4,20},{8,24},{12,28},{16,0},{20,4},{24,8},{28,12},{1,17},{... | collective-permute-start | bytes 3538952 | tf_op jit(solution)/shard_map/ppermute | solution.py:23
  216.3 141.1 %collective-permute-start.3 = (bf16[8,72,512]{2,1,0:T(8,128)(2,1)S(1)}, bf16[8,72,512]{2,1,0:T(8,128)(2,1)}, u32[]{:S(2)}, u32[]{:S(2)}) collective-permute-start(bf16[8,72,512]{2,1,0:T(8,128)(2,1)S(1)} %copy-done.15), channel_id=1, source_target_pairs={{0,16},{4,20},{8,24},{12,28},{16,0},{20,4},{24,8},{28,12},{1,17},{... | collective-permute-start | bytes 1769480 | tf_op jit(solution)/shard_map/ppermute | solution.py:23
  216.8 181.5 %collective-permute-start.12 = (bf16[16,72,512]{2,1,0:T(8,128)(2,1)}, bf16[16,72,512]{2,1,0:T(8,128)(2,1)}, u32[]{:S(2)}, u32[]{:S(2)}) collective-permute-start(bf16[16,72,512]{2,1,0:T(8,128)(2,1)} %copy-done.6), channel_id=1, source_target_pairs={{0,16},{4,20},{8,24},{12,28},{16,0},{20,4},{24,8},{28,12},{1,17},{... | collective-permute-start | bytes 3538952 | tf_op jit(solution)/shard_map/ppermute | solution.py:23
  219.3 176.1 %collective-permute-start.6 = (bf16[8,72,512]{2,1,0:T(8,128)(2,1)S(1)}, bf16[8,72,512]{2,1,0:T(8,128)(2,1)}, u32[]{:S(2)}, u32[]{:S(2)}) collective-permute-start(bf16[8,72,512]{2,1,0:T(8,128)(2,1)S(1)} %copy-done.13), channel_id=1, source_target_pairs={{0,16},{4,20},{8,24},{12,28},{16,0},{20,4},{24,8},{28,12},{1,17},{... | collective-permute-start | bytes 1769480 | tf_op jit(solution)/shard_map/ppermute | solution.py:23
  232.0 22.9 %copy-start.27 = (s32[16]{0:T(128)S(1)}, s32[16]{0:T(128)}, u32[]{:S(2)}) copy-start(s32[16]{0:T(128)} %param.17) | copy-start | bytes 196
  252.5 167.4 %collective-permute-start.15 = (bf16[16,72,512]{2,1,0:T(8,128)(2,1)}, bf16[16,72,512]{2,1,0:T(8,128)(2,1)}, u32[]{:S(2)}, u32[]{:S(2)}) collective-permute-start(bf16[16,72,512]{2,1,0:T(8,128)(2,1)} %physics.9), channel_id=1, source_target_pairs={{0,16},{4,20},{8,24},{12,28},{16,0},{20,4},{24,8},{28,12},{1,17},{... | collective-permute-start | bytes 3538952 | tf_op jit(solution)/shard_map/ppermute | solution.py:23
  400.0 19.9 %copy-start.22 = (bf16[64,72,512]{2,1,0:T(8,128)(2,1)}, bf16[64,72,512]{2,1,0:T(8,128)(2,1)S(1)}, u32[]{:S(2)}) copy-start(bf16[64,72,512]{2,1,0:T(8,128)(2,1)S(1)} %select_dynamic-update-slice_fusion.1) | copy-start | bytes 14155780
  (26 other events, 87.8 us)
